TPU v7x, 512 devices: a whole 4x4x16 slice. The times are simulated.
512 devices in a mesh: dom: 128 (over x, z, core), feat: 4 (over y).
Axes of the slice: x: 4, y: 4, z: 16, core: 2. Of those that a mesh axis runs over, the one named last changes fastest.
Arguments:
- features: bfloat16 [256, 131072], P('feat', 'dom'), may hold values from -6 to 6
- cotangent: bfloat16 [256, 131072], P('feat', 'dom'), may hold values from -6 to 6
- w_self: bfloat16 [256, 256], replicated, may hold values from -0.375 to 0.375
- w_neigh: bfloat16 [256, 256], replicated, may hold values from -0.375 to 0.375
- out_bias: float32 [256], replicated, may hold values from -3 to 3
- local_pairs: int32 [128, 12, 2], P('dom'), may hold values from 0 to 7
- local_tiles: bfloat16 [128, 12, 128, 128], P('dom'), may hold values from -0.3125 to 0.3125
- boundary: int32 [128, 7, 512], P('dom'), may hold values from 0 to 1023, as said below
- cross_dst: int32 [128, 7, 4], P('dom'), may hold values from 0 to 7
- cross_src: int32 [128, 7, 4], P('dom'), may hold values from 0 to 3, as said below
- cross_count: int32 [128, 7], P('dom'), may hold values from 1 to 4, as said below
- cross_tiles: bfloat16 [128, 7, 4, 128, 128], P('dom'), may hold values from -0.3125 to 0.3125
Outputs:
- output: bfloat16 [256, 131072], P('feat', 'dom')
- grad_features: bfloat16 [256, 131072], P('feat', 'dom')
- grad_self: float32 [256, 256], P(None, 'feat')
- grad_neigh: float32 [256, 256], P(None, 'feat')
- grad_bias: float32 [256], P('feat')
Inputs may be any that keep to these rules, and one draw needn't show every extreme that they name: For each owner o and level l, the 512 entries boundary[o, l] are distinct local node numbers of owner o; these are the nodes whose features o sends to its partner o XOR 2^l. `cross_src`: for each owner and level the 4 slots name 4 distinct blocks. Slots of an owner at a level from cross_count on are padding: their tiles and block numbers are ignored.
All inputs are finite; a program needn't handle non-finite values.
Results may differ from a plain program's by a relative error of at most 0.007.
Values may be sent and summed in bfloat16 or wider, within the bound.
A program may use at most 64 MiB of HBM per device.

v0:
```python
import math

import jax
import jax.numpy as jnp
from jax import lax
from jax.sharding import PartitionSpec as P

BLK = 128


def from_partner(block, axis, apart):
    count = lax.axis_size(axis)
    route = []
    for low in range(count):
        high = low | 1 << apart
        if high != low and high < count:
            route += [(low, high), (high, low)]
    return lax.ppermute(block, axis, route)


def silu_slope(values):
    sigma = jax.nn.sigmoid(values)
    return sigma * (1.0 + values * (1.0 - sigma))


def select_blocks(blocks, indices):
    onehot = (indices[:, None] == jnp.arange(blocks.shape[1], dtype=jnp.int32)[None, :]).astype(
        blocks.dtype
    )
    return jnp.einsum("fbk,tb->tfk", blocks, onehot, preferred_element_type=jnp.float32).astype(
        blocks.dtype
    )


def place_blocks(values, indices, put_count):
    onehot = (indices[:, None] == jnp.arange(put_count, dtype=jnp.int32)[None, :]).astype(
        jnp.float32
    )
    return jnp.einsum("tfk,tb->fbk", values, onehot, precision=lax.Precision.HIGHEST)


def apply_tiles(picked, tile_set, forward):
    if forward:
        return jnp.einsum("tfk,tjk->tfj", picked, tile_set, preferred_element_type=jnp.float32)
    return jnp.einsum("tfj,tjk->tfk", picked, tile_set, preferred_element_type=jnp.float32)


def cross_terms(source, pick_index, put_index, put_count, tile_set, live_count, forward):
    products = apply_tiles(select_blocks(source, pick_index), tile_set, forward)
    live_mask = (jnp.arange(tile_set.shape[0], dtype=jnp.int32) < live_count).astype(jnp.float32)
    return place_blocks(products * live_mask[:, None, None], put_index, put_count)


def on_device(
    features,
    cotangent,
    w_self,
    w_neigh,
    out_bias,
    local_pairs,
    local_tiles,
    boundary,
    cross_dst,
    cross_src,
    cross_count,
    cross_tiles,
):
    feat_rows, nodes_here = features.shape
    nblocks = nodes_here // BLK
    owners = lax.axis_size("dom")
    levels = owners.bit_length() - 1
    first_row = lax.axis_index("feat") * feat_rows
    pair_list = local_pairs[0]
    tiles_here = local_tiles[0]
    blocks = features.reshape(feat_rows, nblocks, BLK)
    summed = place_blocks(
        apply_tiles(select_blocks(blocks, pair_list[:, 1]), tiles_here, True),
        pair_list[:, 0],
        nblocks,
    )
    for bit_level in range(levels):
        send_rows = boundary[0, bit_level]
        rblocks = send_rows.shape[0] // BLK
        outgoing = jnp.take(features, send_rows, axis=1)
        incoming = from_partner(outgoing, "dom", bit_level)
        summed = summed + cross_terms(
            incoming.reshape(feat_rows, rblocks, BLK),
            cross_src[0, bit_level],
            cross_dst[0, bit_level],
            nblocks,
            cross_tiles[0, bit_level],
            cross_count[0, bit_level],
            True,
        )
    neighbours = summed.reshape(feat_rows, nodes_here).astype(jnp.bfloat16)
    self_rows = lax.dynamic_slice_in_dim(w_self, first_row, feat_rows, 0)
    neigh_rows = lax.dynamic_slice_in_dim(w_neigh, first_row, feat_rows, 0)
    self_cols = lax.dynamic_slice_in_dim(w_self, first_row, feat_rows, 1)
    neigh_cols = lax.dynamic_slice_in_dim(w_neigh, first_row, feat_rows, 1)
    bias_here = lax.dynamic_slice_in_dim(out_bias, first_row, feat_rows, 0)
    accum = jnp.dot(
        self_rows,
        lax.all_gather(features, "feat", axis=0, tiled=True),
        preferred_element_type=jnp.float32,
    )
    mixed = accum + jnp.dot(
        neigh_rows,
        lax.all_gather(neighbours, "feat", axis=0, tiled=True),
        preferred_element_type=jnp.float32,
    )
    preact = mixed + bias_here[:, None]
    output = jax.nn.silu(preact).astype(jnp.bfloat16)
    slope_rows = (cotangent.astype(jnp.float32) * silu_slope(preact)).astype(jnp.bfloat16)
    slope_all = lax.all_gather(slope_rows, "feat", axis=0, tiled=True)
    dense = jnp.einsum("oi,on->in", self_cols, slope_all, preferred_element_type=jnp.float32)
    upstream = jnp.einsum(
        "oi,on->in", neigh_cols, slope_all, preferred_element_type=jnp.float32
    ).astype(jnp.bfloat16)
    grad_self_part = jnp.einsum(
        "on,in->oi", slope_all, features, preferred_element_type=jnp.float32
    )
    grad_neigh_part = jnp.einsum(
        "on,in->oi", slope_all, neighbours, preferred_element_type=jnp.float32
    )
    bias_part = jnp.sum(slope_rows.astype(jnp.float32), axis=1)
    totals = lax.psum((grad_self_part, grad_neigh_part, bias_part), "dom")
    norm_scale = 1.0 / math.sqrt(nodes_here * owners)
    up_blocks = upstream.reshape(feat_rows, nblocks, BLK)
    spread = place_blocks(
        apply_tiles(select_blocks(up_blocks, pair_list[:, 0]), tiles_here, False),
        pair_list[:, 1],
        nblocks,
    )
    grad_sum = dense + spread.reshape(feat_rows, nodes_here)
    for bit_level in range(levels):
        send_rows = boundary[0, bit_level]
        rblocks = send_rows.shape[0] // BLK
        back_terms = cross_terms(
            up_blocks,
            cross_dst[0, bit_level],
            cross_src[0, bit_level],
            rblocks,
            cross_tiles[0, bit_level],
            cross_count[0, bit_level],
            False,
        )
        returned = from_partner(back_terms.reshape(feat_rows, send_rows.shape[0]), "dom", bit_level)
        grad_sum = grad_sum.at[:, send_rows].add(returned)
    return (
        output,
        grad_sum.astype(jnp.bfloat16),
        totals[0] * norm_scale,
        totals[1] * norm_scale,
        totals[2] * norm_scale,
    )


def solution(mesh):
    placed = (
        P("feat", "dom"),
        P("feat", "dom"),
        P(),
        P(),
        P(),
        P("dom", None, None),
        P("dom", None, None, None),
        P("dom", None, None),
        P("dom", None, None),
        P("dom", None, None),
        P("dom", None),
        P("dom", None, None, None, None),
    )
    return jax.shard_map(
        on_device,
        mesh=mesh,
        in_specs=placed,
        out_specs=(P("feat", "dom"), P("feat", "dom"), P(None, "feat"), P(None, "feat"), P("feat")),
        check_vma=False,
    )
```

profile of v0, /device:TPU:1, one launch (start us, length us, event | category | flops | bytes accessed | tf_op | source)
XLA Modules:
  0.0 772.1 jit_solution(2734362052093954785)
XLA Ops:
  7.2 0.8 fusion.187
  8.1 1.1 copy.33
  9.2 1.3 gather_fusion
  10.5 0.8 select_bitcast_fusion.6
  11.3 8.8 %collective-permute-start = (bf16[64,512]{0,1:T(8,128)(2,1)}, bf16[64,512]{0,1:T(8,128)(2,1)S(1)}, u32[]{:S(2)}, u32[]{:S(2)}) collective-permute-start(bf16[64,512]{0,1:T(8,128)(2,1)} %select_bitcast_fusion.6), channel_id=1, source_target_pairs={{0,4},{4,0},{8,12},{12,8},{16,20},{20,16},{24,28},{28,24},{32,36},... | collective-permute-start | bytes 196616 | tf_op jit(solution)/shard_map/ppermute | solution.py:18
  20.1 1.3 gather_fusion.1
  21.5 0.8 select_bitcast_fusion.5
  22.3 1.9 collective-permute-start.1
  24.2 1.3 gather_fusion.2
  25.6 0.8 select_bitcast_fusion.4
  26.3 1.9 collective-permute-start.2
  28.3 1.3 gather_fusion.3
  29.7 0.8 select_bitcast_fusion.3
  30.4 8.0 %collective-permute-start.3 = (bf16[64,512]{0,1:T(8,128)(2,1)}, bf16[64,512]{0,1:T(8,128)(2,1)S(1)}, u32[]{:S(2)}, u32[]{:S(2)}) collective-permute-start(bf16[64,512]{0,1:T(8,128)(2,1)} %select_bitcast_fusion.3), channel_id=1, source_target_pairs={{0,32},{32,0},{4,36},{36,4},{8,40},{40,8},{12,44},{44,12},{16,48},... | collective-permute-start | bytes 196616 | tf_op jit(solution)/shard_map/ppermute | solution.py:18
  38.5 1.3 gather_fusion.4
  39.9 0.8 select_bitcast_fusion.2
  40.7 7.9 %collective-permute-start.4 = (bf16[64,512]{0,1:T(8,128)(2,1)}, bf16[64,512]{0,1:T(8,128)(2,1)}, u32[]{:S(2)}, u32[]{:S(2)}) collective-permute-start(bf16[64,512]{0,1:T(8,128)(2,1)} %select_bitcast_fusion.2), channel_id=1, source_target_pairs={{0,64},{64,0},{4,68},{68,4},{8,72},{72,8},{12,76},{76,12},{16,80},... | collective-permute-start | bytes 196616 | tf_op jit(solution)/shard_map/ppermute | solution.py:18
  48.7 12.4 %all_gather.9 = bf16[256,1024]{1,0:T(8,128)(2,1)S(1)} all-gather(bf16[64,1024]{1,0:T(8,128)(2,1)S(1)} %copy-done.2), channel_id=1, replica_groups=mesh['dom'=128,'feat'=4] {'feat'}, dimensions={0}, use_global_device_ids=true | all-gather | bytes 655360 | tf_op jit(solution)/shard_map/all_gather | solution.py:103
  61.7 0.8 slice_reduce_fusion
  63.2 1.3 compare_convert_fusion.6
  64.5 0.8 slice_reduce_fusion.1
  66.0 1.2 compare_convert_fusion.5
  67.2 1.1 compare_convert_fusion.4
  68.4 1.2 compare_convert_fusion.3
  69.6 1.2 compare_convert_fusion.2
  70.8 1.3 gather_fusion.5
  72.2 1.2 compare_convert_fusion.1
  73.3 1.3 gather_fusion.6
  75.9 0.8 select_bitcast_fusion.1
  76.7 0.8 select_bitcast_fusion
  78.1 1.0 fusion.84
  79.0 1.1 compare_convert_fusion
  80.2 3.1 collective-permute-start.5
  83.4 4.4 collective-permute-start.6
  91.8 1.0 copy.63
  101.9 10.0 %all_gather.10 = bf16[256,1024]{1,0:T(8,128)(2,1)S(1)} all-gather(bf16[64,1024]{1,0:T(8,128)(2,1)S(1)} %bitcast.257), channel_id=1, replica_groups=mesh['dom'=128,'feat'=4] {'feat'}, dimensions={0}, use_global_device_ids=true | all-gather | bytes 655360 | tf_op jit(solution)/shard_map/all_gather | solution.py:108
  111.9 1.6 convert_reduce_fusion
  113.5 10.1 %all_gather.11 = bf16[256,1024]{1,0:T(8,128)(2,1)S(1)} all-gather(bf16[64,1024]{1,0:T(8,128)(2,1)S(1)} %get-tuple-element.33), channel_id=1, replica_groups=mesh['dom'=128,'feat'=4] {'feat'}, dimensions={0}, use_global_device_ids=true | all-gather | bytes 655360 | tf_op jit(solution)/shard_map/all_gather | solution.py:114
  123.6 0.9 fusion.186
  124.5 0.9 fusion.189
  128.1 0.9 fusion.115
  131.3 0.9 copy.88
  132.2 11.2 %collective-permute-start.7 = (f32[64,512]{0,1:T(8,128)}, f32[64,512]{0,1:T(8,128)S(1)}, u32[]{:S(2)}, u32[]{:S(2)}) collective-permute-start(f32[64,512]{0,1:T(8,128)} %bitcast.60), channel_id=1, source_target_pairs={{0,4},{4,0},{8,12},{12,8},{16,20},{20,16},{24,28},{28,24},{32,36},... | collective-permute-start | bytes 393224 | tf_op jit(solution)/shard_map/ppermute | solution.py:18
  143.9 0.9 copy.89
  144.7 2.6 collective-permute-start.8
  147.9 0.8 copy.90
  148.8 2.7 collective-permute-start.9
  151.9 0.8 copy.91
  152.8 5.3 collective-permute-start.10
  158.6 0.8 copy.92
  159.5 2.0 collective-permute-start.11
  164.2 263.8 %psum.23 = f32[64]{0:T(128)S(1)} all-reduce(f32[64]{0:T(128)S(1)} %copy-done.37), channel_id=1, replica_groups=mesh['dom'=128,'feat'=4] {'dom'}, use_global_device_ids=true, to_apply=%region_10.12 | all-reduce | flops 64 | bytes 512 | tf_op jit(solution)/shard_map/psum | solution.py:126
  429.1 1.9 collective-permute-start.12
  431.0 1.9 collective-permute-start.13
  432.9 304.2 %all-reduce.3.cloned.1.call-done = (f32[256,64]{0,1:T(8,128)}, f32[256,64]{0,1:T(8,128)}) async-done(((f32[256,64]{0,1:T(8,128)}, f32[256,64]{0,1:T(8,128)}), (f32[256,64]{0,1:T(8,128)}, f32[256,64]{0,1:T(8,128)})) %all-reduce.3.cloned.1.call-update) | async-done | bytes 131088 | tf_op jit(solution)/shard_map/psum | solution.py:126
  737.1 1.5 broadcast_multiply_fusion
  738.6 3.6 scatter_custom_fusion
  742.3 3.6 scatter_custom_fusion.1
  745.9 3.9 scatter_custom_fusion.2
  749.8 3.6 scatter_custom_fusion.3
  753.5 3.6 scatter_custom_fusion.4
  757.2 3.6 scatter_custom_fusion.5
  760.8 3.6 scatter_custom_fusion.6
  764.5 0.8 copy.48
  (180 shorter events, 27.5 us)
Async XLA Ops:
  7.2 67.8 %copy-start = (bf16[1,12,128,128]{3,2,1,0:T(8,128)(2,1)S(1)}, bf16[1,12,128,128]{3,2,1,0:T(8,128)(2,1)}, u32[]{:S(2)}) copy-start(bf16[1,12,128,128]{3,2,1,0:T(8,128)(2,1)} %param.20) | copy-start | bytes 1179652
  7.2 729.9 %all-reduce.3.cloned.1.call-start = ((), (), s32[]{:S(2)}) async-start(), calls=%async_computation | async-start | bytes 262144 | tf_op jit(solution)/shard_map/psum | solution.py:126
  11.3 68.9 %collective-permute-start = (bf16[64,512]{0,1:T(8,128)(2,1)}, bf16[64,512]{0,1:T(8,128)(2,1)S(1)}, u32[]{:S(2)}, u32[]{:S(2)}) collective-permute-start(bf16[64,512]{0,1:T(8,128)(2,1)} %select_bitcast_fusion.6), channel_id=1, source_target_pairs={{0,4},{4,0},{8,12},{12,8},{16,20},{20,16},{24,28},{28,24},{32,36},... | collective-permute-start | bytes 196616 | tf_op jit(solution)/shard_map/ppermute | solution.py:18
  22.3 61.1 %collective-permute-start.1 = (bf16[64,512]{0,1:T(8,128)(2,1)}, bf16[64,512]{0,1:T(8,128)(2,1)S(1)}, u32[]{:S(2)}, u32[]{:S(2)}) collective-permute-start(bf16[64,512]{0,1:T(8,128)(2,1)} %select_bitcast_fusion.5), channel_id=1, source_target_pairs={{0,8},{8,0},{4,12},{12,4},{16,24},{24,16},{20,28},{28,20},{32,40},... | collective-permute-start | bytes 196616 | tf_op jit(solution)/shard_map/ppermute | solution.py:18
  26.3 63.7 %collective-permute-start.2 = (bf16[64,512]{0,1:T(8,128)(2,1)}, bf16[64,512]{0,1:T(8,128)(2,1)S(1)}, u32[]{:S(2)}, u32[]{:S(2)}) collective-permute-start(bf16[64,512]{0,1:T(8,128)(2,1)} %select_bitcast_fusion.4), channel_id=1, source_target_pairs={{0,16},{16,0},{4,20},{20,4},{8,24},{24,8},{12,28},{28,12},{32,48},... | collective-permute-start | bytes 196616 | tf_op jit(solution)/shard_map/ppermute | solution.py:18
  30.4 60.8 %collective-permute-start.3 = (bf16[64,512]{0,1:T(8,128)(2,1)}, bf16[64,512]{0,1:T(8,128)(2,1)S(1)}, u32[]{:S(2)}, u32[]{:S(2)}) collective-permute-start(bf16[64,512]{0,1:T(8,128)(2,1)} %select_bitcast_fusion.3), channel_id=1, source_target_pairs={{0,32},{32,0},{4,36},{36,4},{8,40},{40,8},{12,44},{44,12},{16,48},... | collective-permute-start | bytes 196616 | tf_op jit(solution)/shard_map/ppermute | solution.py:18
  39.9 8.8 %copy-start.2 = (bf16[64,1024]{1,0:T(8,128)(2,1)S(1)}, bf16[64,1024]{1,0:T(8,128)(2,1)}, u32[]{:S(2)}) copy-start(bf16[64,1024]{1,0:T(8,128)(2,1)} %param.14) | copy-start | bytes 393220
  40.7 51.1 %collective-permute-start.4 = (bf16[64,512]{0,1:T(8,128)(2,1)}, bf16[64,512]{0,1:T(8,128)(2,1)}, u32[]{:S(2)}, u32[]{:S(2)}) collective-permute-start(bf16[64,512]{0,1:T(8,128)(2,1)} %select_bitcast_fusion.2), channel_id=1, source_target_pairs={{0,64},{64,0},{4,68},{68,4},{8,72},{72,8},{12,76},{76,12},{16,80},... | collective-permute-start | bytes 196616 | tf_op jit(solution)/shard_map/ppermute | solution.py:18
  48.7 12.4 %copy-start.7 = (s32[1,7,512]{2,0,1:T(1,128)S(1)}, s32[1,7,512]{2,0,1:T(1,128)}, u32[]{:S(2)}) copy-start(s32[1,7,512]{2,0,1:T(1,128)} %param.21) | copy-start | bytes 43012
  48.7 13.0 %copy-start.4 = (s32[1,7,4]{1,2,0:T(4,128)S(1)}, s32[1,7,4]{1,2,0:T(4,128)}, u32[]{:S(2)}) copy-start(s32[1,7,4]{1,2,0:T(4,128)} %param.23) | copy-start | bytes 340
  48.7 13.8 %copy-start.9 = (s32[1,7]{1,0:T(1,128)S(1)}, s32[1,7]{1,0:T(1,128)}, u32[]{:S(2)}) copy-start(s32[1,7]{1,0:T(1,128)} %param.24) | copy-start | bytes 88
  63.2 1.3 copy-start.5
  65.3 0.7 copy-start.33
  66.0 8.7 %copy-start.20 = (s32[12]{0:T(128)}, s32[12]{0:T(128)S(1)}, u32[]{:S(2)}) copy-start(s32[12]{0:T(128)S(1)} %get-tuple-element.50) | copy-start | bytes 148
  66.0 9.4 %copy-start.22 = (s32[12]{0:T(128)}, s32[12]{0:T(128)S(1)}, u32[]{:S(2)}) copy-start(s32[12]{0:T(128)S(1)} %get-tuple-element.49) | copy-start | bytes 148
  75.4 2.1 copy-start.35
  75.9 12.8 %copy-start.1 = (bf16[1,7,4,128,128]{4,3,2,1,0:T(8,128)(2,1)S(1)}, bf16[1,7,4,128,128]{4,3,2,1,0:T(8,128)(2,1)}, u32[]{:S(2)}) copy-start(bf16[1,7,4,128,128]{4,3,2,1,0:T(8,128)(2,1)} %param.25) | copy-start | bytes 2752516
  80.2 13.1 %collective-permute-start.5 = (bf16[64,512]{0,1:T(8,128)(2,1)}, bf16[64,512]{0,1:T(8,128)(2,1)S(1)}, u32[]{:S(2)}, u32[]{:S(2)}) collective-permute-start(bf16[64,512]{0,1:T(8,128)(2,1)} %select_bitcast_fusion.1), channel_id=1, source_target_pairs={{0,128},{128,0},{4,132},{132,4},{8,136},{136,8},{12,140},{140,12},... | collective-permute-start | bytes 196616 | tf_op jit(solution)/shard_map/ppermute | solution.py:18
  83.4 10.4 %collective-permute-start.6 = (bf16[64,512]{0,1:T(8,128)(2,1)}, bf16[64,512]{0,1:T(8,128)(2,1)S(1)}, u32[]{:S(2)}, u32[]{:S(2)}) collective-permute-start(bf16[64,512]{0,1:T(8,128)(2,1)} %select_bitcast_fusion), channel_id=1, source_target_pairs={{0,256},{256,0},{4,260},{260,4},{8,264},{264,8},{12,268},{268,12},... | collective-permute-start | bytes 196616 | tf_op jit(solution)/shard_map/ppermute | solution.py:18
  87.9 0.6 copy-start.12
  88.9 0.7 copy-start.11
  90.2 0.7 copy-start.10
  94.4 0.7 copy-start.18
  94.4 0.7 copy-start.29
  95.5 0.6 copy-start.17
  95.5 0.7 copy-start.30
  96.5 0.7 copy-start.16
  96.5 0.7 copy-start.28
  97.6 0.6 copy-start.15
  97.6 0.6 copy-start.27
  98.6 0.7 copy-start.14
  98.7 0.7 copy-start.26
  99.7 0.6 copy-start.13
  99.7 0.6 copy-start.24
  100.8 0.6 copy-start.19
  100.8 0.7 copy-start.31
  101.9 10.1 %copy-start.8 = (bf16[256,256]{1,0:T(8,128)(2,1)S(1)}, bf16[256,256]{1,0:T(8,128)(2,1)}, u32[]{:S(2)}) copy-start(bf16[256,256]{1,0:T(8,128)(2,1)} %param.17) | copy-start | bytes 393220
  101.9 10.1 %copy-start.34 = (bf16[64,1024]{1,0:T(8,128)(2,1)S(1)}, bf16[64,1024]{1,0:T(8,128)(2,1)}, u32[]{:S(2)}) copy-start(bf16[64,1024]{1,0:T(8,128)(2,1)} %param.15) | copy-start | bytes 393220
  101.9 10.1 %copy-start.36 = (f32[64]{0:T(128)S(1)}, f32[64]{0:T(128)}, u32[]{:S(2)}) copy-start(f32[64]{0:T(128)} %dynamic_slice.17) | copy-start | bytes 772
  125.8 0.6 copy-start.23
  128.9 0.7 copy-start.21
  129.6 0.9 copy-start.6
  132.2 296.9 %collective-permute-start.7 = (f32[64,512]{0,1:T(8,128)}, f32[64,512]{0,1:T(8,128)S(1)}, u32[]{:S(2)}, u32[]{:S(2)}) collective-permute-start(f32[64,512]{0,1:T(8,128)} %bitcast.60), channel_id=1, source_target_pairs={{0,4},{4,0},{8,12},{12,8},{16,20},{20,16},{24,28},{28,24},{32,36},... | collective-permute-start | bytes 393224 | tf_op jit(solution)/shard_map/ppermute | solution.py:18
  144.7 286.3 %collective-permute-start.8 = (f32[64,512]{0,1:T(8,128)}, f32[64,512]{0,1:T(8,128)S(1)}, u32[]{:S(2)}, u32[]{:S(2)}) collective-permute-start(f32[64,512]{0,1:T(8,128)} %bitcast.65), channel_id=1, source_target_pairs={{0,8},{8,0},{4,12},{12,4},{16,24},{24,16},{20,28},{28,20},{32,40},... | collective-permute-start | bytes 393224 | tf_op jit(solution)/shard_map/ppermute | solution.py:18
  148.8 597.2 %collective-permute-start.9 = (f32[64,512]{0,1:T(8,128)}, f32[64,512]{0,1:T(8,128)S(1)}, u32[]{:S(2)}, u32[]{:S(2)}) collective-permute-start(f32[64,512]{0,1:T(8,128)} %bitcast.70), channel_id=1, source_target_pairs={{0,16},{16,0},{4,20},{20,4},{8,24},{24,8},{12,28},{28,12},{32,48},... | collective-permute-start | bytes 393224 | tf_op jit(solution)/shard_map/ppermute | solution.py:18
  152.8 597.0 %collective-permute-start.10 = (f32[64,512]{0,1:T(8,128)}, f32[64,512]{0,1:T(8,128)S(1)}, u32[]{:S(2)}, u32[]{:S(2)}) collective-permute-start(f32[64,512]{0,1:T(8,128)} %bitcast.75), channel_id=1, source_target_pairs={{0,32},{32,0},{4,36},{36,4},{8,40},{40,8},{12,44},{44,12},{16,48},... | collective-permute-start | bytes 393224 | tf_op jit(solution)/shard_map/ppermute | solution.py:18
  159.5 2.2 copy-start.25
  159.5 594.0 %collective-permute-start.11 = (f32[64,512]{0,1:T(8,128)}, f32[64,512]{0,1:T(8,128)S(1)}, u32[]{:S(2)}, u32[]{:S(2)}) collective-permute-start(f32[64,512]{0,1:T(8,128)} %bitcast.80), channel_id=1, source_target_pairs={{0,64},{64,0},{4,68},{68,4},{8,72},{72,8},{12,76},{76,12},{16,80},... | collective-permute-start | bytes 393224 | tf_op jit(solution)/shard_map/ppermute | solution.py:18
  161.7 0.9 copy-start.3
  162.5 0.7 copy-start.32
  163.5 0.7 copy-start.37
  429.1 328.1 %collective-permute-start.12 = (f32[64,512]{0,1:T(8,128)S(1)}, f32[64,512]{0,1:T(8,128)S(1)}, u32[]{:S(2)}, u32[]{:S(2)}) collective-permute-start(f32[64,512]{0,1:T(8,128)S(1)} %bitcast.260), channel_id=1, source_target_pairs={{0,128},{128,0},{4,132},{132,4},{8,136},{136,8},{12,140},{140,12},... | collective-permute-start | bytes 393224 | tf_op jit(solution)/shard_map/ppermute | solution.py:18
  431.0 329.8 %collective-permute-start.13 = (f32[64,512]{0,1:T(8,128)S(1)}, f32[64,512]{0,1:T(8,128)S(1)}, u32[]{:S(2)}, u32[]{:S(2)}) collective-permute-start(f32[64,512]{0,1:T(8,128)S(1)} %bitcast.259), channel_id=1, source_target_pairs={{0,256},{256,0},{4,260},{260,4},{8,264},{264,8},{12,268},{268,12},... | collective-permute-start | bytes 393224 | tf_op jit(solution)/shard_map/ppermute | solution.py:18
Sparse Core Ops, SparseCore 0:
  428.2 308.8 all-reduce.2
where the time goes:
time: 774 us; the launch traced here: 772 us
  waiting for transfers between devices  304 us (39%)
  blocking collectives  296 us (38%)
  starting transfers between devices  63.7 us (8%)
  other arithmetic  42.4 us (5%)
  local copies, waits for them, and re-layouts  31.8 us (4%)
  matrix products  18.5 us (2%)
  between operations  15.2 us (2%)
    psum x1, waiting for transfers between devices, on_device(): totals = lax.psum((grad_self_part, grad_neigh_part, bias_part), 'dom')  304 us
    psum x1, blocking collectives, on_device(): totals = lax.psum((grad_self_part, grad_neigh_part, bias_part), 'dom')  264 us
    ppermute x14, starting transfers between devices, from_partner(): return lax.ppermute(block, axis, route)  63.7 us
    scatter-add x7, other arithmetic, on_device(): grad_sum = grad_sum.at[:, send_rows].add(returned)  25.7 us
  transfers between devices with their start and end apart: 15, of which 1 were waited for; matrix products, arithmetic and copies ran while one was open for 8% of the time, Pallas kernels for 0%

commit v1 on v0

v1 whole, which is shorter than its diff:
```python
import functools
import math

import jax
import jax.numpy as jnp
from jax import lax
from jax.experimental import pallas as pl
from jax.experimental.pallas import tpu as pltpu
from jax.sharding import PartitionSpec as P

MESH = pl.DeviceIdType.MESH
BF16 = jnp.bfloat16
F32 = jnp.float32

BLK = 128
NB = 8
CT = 4
NLT = 12
LEVELS = 7
XS, ZS, YS = 4, 16, 4
FL = 64
GROUP = 2 * XS
SEND_ORDER = (4, 3, 2, 6, 1, 5, 0)
TAKE_ORDER = (0, 5, 1, 6, 2, 3, 4)
N_COPIES = 2 * LEVELS + 7 * (YS - 1) + 2 * (GROUP - 1) + 9


def nt(a, b):
    return lax.dot_general(a, b, (((1,), (1,)), ((), ())), preferred_element_type=F32)


def nn(a, b):
    return lax.dot_general(a, b, (((1,), (0,)), ((), ())), preferred_element_type=F32)


def kernel(
    scale,
    pairs, cdst, csrc, ccnt,
    feat, cot, w_self, w_neigh, bias, bound, ltile, ctile,
    out, gfeat, gself, gneigh, gbias,
    onehot, fb, cb, xs, xr0, xr1, xr2, xr3, xr4, xr5, xr6, bs, br, acc, gacc, fa, cot3, agg, wp, wpt, bcol,
    sl3, o3, outr, du, upr, dnr, gf, gs, gr, cs, cr, zs, zr, us, ur, pg, full,
    send, recv,
):
    xr = (xr0, xr1, xr2, xr3, xr4, xr5, xr6)
    y = lax.axis_index("feat")
    o = lax.axis_index("dom")
    core = lax.rem(o, 2)
    z = lax.rem(lax.div(o, 2), ZS)
    x = lax.div(o, 2 * ZS)
    zl = lax.rem(z, 4)
    zh = lax.div(z, 4)
    g = x * 2 + core

    def at(g_, z_):
        return lax.div(g_, 2) * (2 * ZS) + z_ * 2 + lax.rem(g_, 2)

    def partner(level):
        step = 1 << level
        return o + step * (1 - 2 * lax.rem(lax.div(o, step), 2))

    y_to = [lax.rem(y + k, YS) for k in range(YS)]
    y_from = [lax.rem(y + YS - k, YS) for k in range(YS)]
    g_to = [lax.rem(g + k, GROUP) for k in range(GROUP)]
    g_from = [lax.rem(g + GROUP - k, GROUP) for k in range(GROUP)]
    zl_to = [lax.rem(zl + k, 4) for k in range(4)]
    zl_from = [lax.rem(zl + 4 - k, 4) for k in range(4)]
    zh_to = [lax.rem(zh + k, 4) for k in range(4)]

    y_dev = [{"feat": y_to[k]} for k in range(YS)]
    g_dev = [{"dom": at(g_to[k], z)} for k in range(GROUP)]
    zl_dev = [{"dom": at(g, zh * 4 + zl_to[k])} for k in range(4)]
    zh_dev = [{"dom": at(g, zh_to[k] * 4 + zl)} for k in range(4)]

    barrier = pltpu.get_barrier_semaphore()
    greeted = y_dev[1:] + g_dev[1:] + zl_dev[1:] + zh_dev[1:]
    for dev in greeted:
        pl.semaphore_signal(barrier, inc=1, device_id=dev, device_id_type=MESH)

    counter = [0]
    sent = []

    def push(src, dst, landing, dev):
        n = counter[0]
        counter[0] += 1
        copy = pltpu.make_async_remote_copy(
            src_ref=src, dst_ref=dst, send_sem=send.at[n], recv_sem=recv.at[n],
            device_id=dev, device_id_type=MESH,
        )
        copy.start()
        sent.append(copy)
        return pltpu.make_async_remote_copy(
            src_ref=src, dst_ref=landing, send_sem=send.at[n], recv_sem=recv.at[n],
            device_id=dev, device_id_type=MESH,
        )

    def rows(start, size):
        return pl.ds(pl.multiple_of(start, size), size)

    for b in range(NB):
        fb[b] = feat[:, b * BLK:(b + 1) * BLK]
        cb[b] = cot[:, b * BLK:(b + 1) * BLK]

    def gather(level):
        wanted = bound[level]

        def build(i, carry):
            start = pl.multiple_of(i * 64, 64)
            node = lax.broadcasted_iota(jnp.int32, (64, CT * BLK), 0) + start
            onehot[level, pl.ds(start, 64), :] = jnp.where(node == wanted, 1.0, 0.0).astype(BF16)
            return carry

        lax.fori_loop(0, NB * BLK // 64, build, 0)
        picked = nn(feat[...], onehot[level]).astype(BF16)
        for k in range(CT):
            xs[level, k] = picked[:, k * BLK:(k + 1) * BLK]

    def send_level(level, src, dst):
        return push(src, dst, dst, {"dom": partner(level)})

    gather(SEND_ORDER[0])
    pl.semaphore_wait(barrier, len(greeted))

    forward = {SEND_ORDER[0]: send_level(SEND_ORDER[0], xs.at[SEND_ORDER[0]], xr[SEND_ORDER[0]])}
    early = []
    for k in range(1, YS):
        early.append(push(
            fb.at[pl.ds(2 * y_to[k], 2)], fa.at[:, rows(y * 128, 64), :],
            fa.at[:, rows(y_from[k] * 128, 64), :], y_dev[k]))
        early.append(push(
            cb.at[pl.ds(2 * y_to[k], 2)], cot3.at[:, rows(y * 64, 64), :],
            cot3.at[:, rows(y_from[k] * 64, 64), :], y_dev[k]))
    for level in SEND_ORDER[1:]:
        gather(level)
        forward[level] = send_level(level, xs.at[level], xr[level])

    for b in range(2):
        fa[b, rows(y * 128, 64), :] = fb[2 * y + b]
        cot3[b, rows(y * 64, 64), :] = cb[2 * y + b]

    def place(products, targets, lives):
        def one(b, carry):
            total = acc[b]
            for product, target, live in zip(products, targets, lives):
                total = total + product * jnp.where(target == b, live, 0.0)
            acc[b] = total
            return carry

        lax.fori_loop(0, NB, one, 0)

    acc[...] = jnp.zeros_like(acc)
    for first in range(0, NLT, 4):
        tiles = range(first, first + 4)
        place(
            [nt(fb[pairs[1, t]], ltile[t]) for t in tiles],
            [pairs[0, t] for t in tiles],
            [jnp.float32(1.0)] * 4,
        )

    row = lax.broadcasted_iota(jnp.int32, (512, 256), 0)
    col = lax.broadcasted_iota(jnp.int32, (512, 256), 1)
    spot = (col >> 6) * 128 + (col & 63)
    put_self = jnp.where(row == spot, 1.0, 0.0).astype(BF16)
    put_neigh = jnp.where(row == spot + 64, 1.0, 0.0).astype(BF16)
    wp[...] = (nt(w_self[...], put_self) + nt(w_neigh[...], put_neigh)).astype(BF16)
    wpt[...] = (nt(put_self, w_self[...]) + nt(put_neigh, w_neigh[...])).astype(BF16)
    row = lax.broadcasted_iota(jnp.int32, (256, 256), 0)
    col = lax.broadcasted_iota(jnp.int32, (256, 256), 1)
    column = jnp.sum(jnp.where(row == col, bias[...], 0.0), axis=1, keepdims=True)
    bcol[...] = jnp.broadcast_to(column, (256, 128))

    def live_of(level, slot):
        return jnp.where(slot < ccnt[0, level], 1.0, 0.0)

    for level in TAKE_ORDER:
        forward[level].wait_recv()
        place(
            [nt(xr[level][csrc[c, level]], ctile[level * CT + c]) for c in range(CT)],
            [cdst[c, level] for c in range(CT)],
            [live_of(level, c) for c in range(CT)],
        )

    agg[...] = acc[...].astype(BF16)
    waits = []
    for k in range(1, YS):
        waits.append(push(
            agg.at[pl.ds(2 * y_to[k], 2)], fa.at[:, rows(y * 128 + 64, 64), :],
            fa.at[:, rows(y_from[k] * 128 + 64, 64), :], y_dev[k]))
    for b in range(2):
        fa[b, rows(y * 128 + 64, 64), :] = agg[2 * y + b]
    for wait in early + waits:
        wait.wait_recv()

    for b in range(2):
        preact = nn(wp[...], fa[b]) + bcol[...]
        sigma = jax.nn.sigmoid(preact)
        o3[b] = (preact * sigma).astype(BF16)
        slope = sigma * (1.0 + preact * (1.0 - sigma))
        sl3[b] = (cot3[b].astype(F32) * slope).astype(BF16)
    for b in range(2):
        du[b] = nn(wpt[...], sl3[b]).astype(BF16)

    up_waits, late = [], []
    for k in range(1, YS):
        up_waits.append(push(
            du.at[:, rows(y_to[k] * 128 + 64, 64), :], upr.at[pl.ds(2 * y, 2)],
            upr.at[pl.ds(2 * y_from[k], 2)], y_dev[k]))

    for half in range(2):
        total = sum(nt(fa[b], sl3[b, half * 128:(half + 1) * 128, :]) for b in range(2))
        for k in range(YS):
            gf[k, half * 128:(half + 1) * 128, :] = total[k * 128:(k + 1) * 128]
    ones = jnp.ones((16, 128), BF16)
    blank = jnp.zeros((64, 128), BF16)
    for k in range(YS):
        gf[k, 256:272, :] = sum(
            nt(ones, jnp.concatenate([sl3[b, k * 64:(k + 1) * 64, :], blank], axis=0)) for b in range(2)
        )
    gs[...] = gf[...].astype(BF16)
    grad_waits = []
    for k in range(1, YS):
        grad_waits.append(push(gs.at[y_to[k]], gr.at[k - 1], gr.at[k - 1], y_dev[k]))

    for b in range(2):
        upr[2 * y + b] = du[b, rows(y * 128 + 64, 64), :]
    for wait in up_waits:
        wait.wait_recv()

    backward = {}
    for level in SEND_ORDER:
        for k in range(CT):
            slot = CT - 1
            for c in range(CT - 1):
                slot = jnp.where(csrc[c, level] == k, c, slot)
            term = nn(upr[cdst[slot, level]], ctile[level * CT + slot])
            bs[level, k] = (term * live_of(level, slot)).astype(BF16)
        backward[level] = send_level(level, bs.at[level], br.at[level])

    for k in range(1, YS):
        late.append(push(
            o3.at[:, rows(y_to[k] * 64, 64), :], outr.at[pl.ds(2 * y, 2)],
            outr.at[pl.ds(2 * y_from[k], 2)], y_dev[k]))
        late.append(push(
            du.at[:, rows(y_to[k] * 128, 64), :], dnr.at[pl.ds(2 * y, 2)],
            dnr.at[pl.ds(2 * y_from[k], 2)], y_dev[k]))
    for b in range(2):
        outr[2 * y + b] = o3[b, rows(y * 64, 64), :]
        dnr[2 * y + b] = du[b, rows(y * 128, 64), :]

    for wait in grad_waits:
        wait.wait_recv()
    part = gf[y]
    for k in range(YS - 1):
        part = part + gr[k].astype(F32)
    for k in range(GROUP):
        cs[k, 0:32, :] = part[k * 32:(k + 1) * 32]
        cs[k, 32:40, :] = part[256:264]
    grad_waits = [
        push(cs.at[g_to[k]], cr.at[k - 1], cr.at[k - 1], g_dev[k]) for k in range(1, GROUP)
    ]

    acc[...] = jnp.zeros_like(acc)
    for first in range(0, NLT, 4):
        tiles = range(first, first + 4)
        place(
            [nn(upr[pairs[0, t]], ltile[t]) for t in tiles],
            [pairs[1, t] for t in tiles],
            [jnp.float32(1.0)] * 4,
        )

    for wait in grad_waits:
        wait.wait_recv()
    part = cs[g]
    for k in range(GROUP - 1):
        part = part + cr[k]
    for k in range(4):
        zs[k, 0:8, :] = part[k * 8:(k + 1) * 8]
        zs[k, 8:16, :] = part[32:40]
    grad_waits = [push(zs.at[zl_to[k]], zr.at[k - 1], zr.at[k - 1], zl_dev[k]) for k in range(1, 4)]

    def take_back(level):
        backward[level].wait_recv()
        terms = jnp.concatenate([br[level, k] for k in range(CT)], axis=1)
        gacc[...] += nt(terms, onehot[level])

    gacc[...] = jnp.zeros_like(gacc)
    take_back(TAKE_ORDER[0])

    for wait in grad_waits:
        wait.wait_recv()
    us[...] = zs[zl] + zr[0] + zr[1] + zr[2]
    grad_waits = [push(us, ur.at[k - 1], ur.at[k - 1], zh_dev[k]) for k in range(1, 4)]

    take_back(TAKE_ORDER[1])

    for wait in grad_waits:
        wait.wait_recv()
    tile = (us[...] + ur[0] + ur[1] + ur[2]) * scale
    pg[zl] = tile[0:8]
    gbias[...] = tile[8:9, 0:64]
    grad_waits = [push(pg.at[zl], pg.at[zl], pg.at[zl_from[k]], zl_dev[k]) for k in range(1, 4)]

    take_back(TAKE_ORDER[2])

    for wait in grad_waits:
        wait.wait_recv()
    full[g] = pg[...]
    grad_waits = [push(full.at[g], full.at[g], full.at[g_from[k]], g_dev[k]) for k in range(1, GROUP)]

    for wait in late:
        wait.wait_recv()
    for b in range(NB):
        out[:, b * BLK:(b + 1) * BLK] = outr[b]
        acc[b] = acc[b] + dnr[b].astype(F32)

    for level in TAKE_ORDER[3:]:
        take_back(level)
    for b in range(NB):
        lanes = slice(b * BLK, (b + 1) * BLK)
        gfeat[:, lanes] = (gacc[:, lanes] + acc[b]).astype(BF16)

    for wait in grad_waits:
        wait.wait_recv()
    for half in range(2):
        for k in range(4):
            lanes = slice(half * 128, (half + 1) * 128)
            dst = gself if k < 2 else gneigh
            for p in range(4):
                first = (k % 2) * 32 + p * 8
                dst[first:first + 8, lanes] = full[half * 4 + k, p]

    for copy in sent:
        copy.wait_send()


def on_device(
    features, cotangent, w_self, w_neigh, out_bias, local_pairs, local_tiles,
    boundary, cross_dst, cross_src, cross_count, cross_tiles,
):
    nodes = features.shape[1] * lax.axis_size("dom")
    vmem = pl.BlockSpec(memory_space=pltpu.VMEM)
    smem = pl.BlockSpec(memory_space=pltpu.SMEM)
    blocks = (NB, FL, BLK)
    results = pl.pallas_call(
        functools.partial(kernel, 1.0 / math.sqrt(nodes)),
        out_shape=(
            jax.ShapeDtypeStruct((FL, NB * BLK), BF16),
            jax.ShapeDtypeStruct((FL, NB * BLK), BF16),
            jax.ShapeDtypeStruct((FL, 256), F32),
            jax.ShapeDtypeStruct((FL, 256), F32),
            jax.ShapeDtypeStruct((1, FL), F32),
        ),
        in_specs=[smem] * 4 + [vmem] * 8,
        out_specs=(vmem,) * 5,
        scratch_shapes=[
            pltpu.VMEM((LEVELS, NB * BLK, CT * BLK), BF16),
            pltpu.VMEM(blocks, BF16),
            pltpu.VMEM(blocks, BF16),
            pltpu.VMEM((LEVELS, CT, FL, BLK), BF16),
            *[pltpu.VMEM((CT, FL, BLK), BF16)] * LEVELS,
            pltpu.VMEM((LEVELS, CT, FL, BLK), BF16),
            pltpu.VMEM((LEVELS, CT, FL, BLK), BF16),
            pltpu.VMEM(blocks, F32),
            pltpu.VMEM((FL, NB * BLK), F32),
            pltpu.VMEM((2, 512, BLK), BF16),
            pltpu.VMEM((2, 256, BLK), BF16),
            pltpu.VMEM(blocks, BF16),
            pltpu.VMEM((256, 512), BF16),
            pltpu.VMEM((512, 256), BF16),
            pltpu.VMEM((256, BLK), F32),
            pltpu.VMEM((2, 256, BLK), BF16),
            pltpu.VMEM((2, 256, BLK), BF16),
            pltpu.VMEM(blocks, BF16),
            pltpu.VMEM((2, 512, BLK), BF16),
            pltpu.VMEM(blocks, BF16),
            pltpu.VMEM(blocks, BF16),
            pltpu.VMEM((YS, 272, BLK), F32),
            pltpu.VMEM((YS, 272, BLK), BF16),
            pltpu.VMEM((YS - 1, 272, BLK), BF16),
            pltpu.VMEM((GROUP, 40, BLK), F32),
            pltpu.VMEM((GROUP - 1, 40, BLK), F32),
            pltpu.VMEM((4, 16, BLK), F32),
            pltpu.VMEM((3, 16, BLK), F32),
            pltpu.VMEM((16, BLK), F32),
            pltpu.VMEM((3, 16, BLK), F32),
            pltpu.VMEM((4, 8, BLK), F32),
            pltpu.VMEM((GROUP, 4, 8, BLK), F32),
            pltpu.SemaphoreType.DMA((N_COPIES,)),
            pltpu.SemaphoreType.DMA((N_COPIES,)),
        ],
        compiler_params=pltpu.CompilerParams(
            collective_id=0, has_side_effects=True, vmem_limit_bytes=40 * 1024 * 1024
        ),
    )(
        local_pairs[0].T,
        cross_dst[0].T,
        cross_src[0].T,
        cross_count,
        features,
        cotangent,
        w_self,
        w_neigh,
        out_bias.reshape(1, -1),
        boundary.reshape(LEVELS, 1, CT * BLK),
        local_tiles[0],
        cross_tiles.reshape(LEVELS * CT, BLK, BLK),
    )
    out, gfeat, gself, gneigh, gbias = results
    return out, gfeat, gself.T, gneigh.T, gbias.reshape(FL)


def solution(mesh):
    placed = (
        P("feat", "dom"),
        P("feat", "dom"),
        P(),
        P(),
        P(),
        P("dom", None, None),
        P("dom", None, None, None),
        P("dom", None, None),
        P("dom", None, None),
        P("dom", None, None),
        P("dom", None),
        P("dom", None, None, None, None),
    )
    return jax.shard_map(
        on_device,
        mesh=mesh,
        in_specs=placed,
        out_specs=(P("feat", "dom"), P("feat", "dom"), P(None, "feat"), P(None, "feat"), P("feat")),
        check_vma=False,
    )
```

time: 774 us -> 79.6 us (0.10)
  waiting for transfers between devices: 304 us -> 0 us
  blocking collectives: 296 us -> 0 us
  Pallas kernels: 0 us -> 68.3 us
  starting transfers between devices: 63.7 us -> 0 us
  other arithmetic: 42.4 us -> 0 us
  local copies, waits for them, and re-layouts: 31.8 us -> 10.3 us
  matrix products: 18.5 us -> 0 us
  between operations: 15.2 us -> 0.7 us
    psum x1 -> x0, waiting for transfers between devices: 304 us -> none  [on_device(): totals = lax.psum((grad_self_part, grad_neigh_part, bias_part), 'dom')]
    psum x1 -> x0, blocking collectives: 264 us -> none  [on_device(): totals = lax.psum((grad_self_part, grad_neigh_part, bias_part), 'dom')]
    pallas_call x0 -> x1, Pallas kernels: none -> 68.3 us  [on_device(): pl.pallas_call(functools.partial(kernel, 1.0 / math.sqrt(nodes)), out_sha...]
    ppermute x14 -> x0, starting transfers between devices: 63.7 us -> none  [from_partner(): return lax.ppermute(block, axis, route)]
    all_gather x3 -> x0, blocking collectives: 32.5 us -> none  [the longest x1 12.4 us: on_device(): lax.all_gather(features, 'feat', axis=0, tiled=True)]
    scatter-add x7 -> x0, other arithmetic: 25.7 us -> none  [on_device(): grad_sum = grad_sum.at[:, send_rows].add(returned)]
    dot_general x54 -> x0, matrix products: 18.5 us -> none  [the longest x16 6.23 us: place_blocks(): jnp.einsum('tfk,tb->fbk', values, onehot, precision=lax.Precision.HIGHEST)]
    gather x7 -> x0, local copies, waits for them, and re-layouts: 9.37 us -> none  [on_device(): outgoing = jnp.take(features, send_rows, axis=1)]
  transfers between devices with their start and end apart: 15 -> 0, of which waited for: 1 -> 0; matrix products, arithmetic and copies ran while one was open for 8% -> 0% of each run, Pallas kernels for 0% -> 0%
where the time goes in v1:
time: 79.6 us; the launch traced here: 79.3 us
  Pallas kernels  68.3 us (86%)
  local copies, waits for them, and re-layouts  10.3 us (13%)
    pallas_call x1, Pallas kernels, on_device(): pl.pallas_call(functools.partial(kernel, 1.0 / math.sqrt(nodes)), out_sha...  68.3 us
    unnamed x29, local copies, waits for them, and re-layouts  10.3 us

profile of v1, /device:TPU:1, one launch (start us, length us, event | category | flops | bytes accessed | tf_op | source)
XLA Modules:
  0.0 79.3 jit_solution(18376222824417801167)
XLA Ops:
  0.6 0.0 copy-start.10
  0.6 0.0 copy-start.8
  0.7 0.0 copy-start.7
  0.7 0.0 copy-start.9
  0.7 0.0 copy-start.11
  0.7 0.6 copy-done.10
  1.3 0.0 copy-done.8
  1.3 0.0 copy-done.7
  1.4 0.0 copy-done.9
  1.4 0.0 copy-done.11
  1.4 0.0 copy-start
  1.4 1.2 %copy-done = bf16[1,7,4,128,128]{4,3,2,1,0:T(8,128)(2,1)S(1)} copy-done((bf16[1,7,4,128,128]{4,3,2,1,0:T(8,128)(2,1)S(1)}, bf16[1,7,4,128,128]{4,3,2,1,0:T(8,128)(2,1)}, u32[]{:S(2)}) %copy-start) | copy-done | bytes 917528
  2.5 0.0 copy-start.1
  2.5 1.0 %copy-done.1 = bf16[1,12,128,128]{3,2,1,0:T(8,128)(2,1)S(1)} copy-done((bf16[1,12,128,128]{3,2,1,0:T(8,128)(2,1)S(1)}, bf16[1,12,128,128]{3,2,1,0:T(8,128)(2,1)}, u32[]{:S(2)}) %copy-start.1) | copy-done | bytes 393240
  3.5 0.0 copy-start.2
  3.5 0.9 %copy-done.2 = bf16[64,1024]{1,0:T(8,128)(2,1)S(1)} copy-done((bf16[64,1024]{1,0:T(8,128)(2,1)S(1)}, bf16[64,1024]{1,0:T(8,128)(2,1)}, u32[]{:S(2)}) %copy-start.2) | copy-done | bytes 131096
  4.4 0.0 copy-start.3
  4.4 0.9 %copy-done.3 = bf16[64,1024]{1,0:T(8,128)(2,1)S(1)} copy-done((bf16[64,1024]{1,0:T(8,128)(2,1)S(1)}, bf16[64,1024]{1,0:T(8,128)(2,1)}, u32[]{:S(2)}) %copy-start.3) | copy-done | bytes 131096
  5.4 0.0 copy-start.4
  5.4 0.9 %copy-done.4 = bf16[256,256]{1,0:T(8,128)(2,1)S(1)} copy-done((bf16[256,256]{1,0:T(8,128)(2,1)S(1)}, bf16[256,256]{1,0:T(8,128)(2,1)}, u32[]{:S(2)}) %copy-start.4) | copy-done | bytes 131096
  6.3 0.0 copy-start.5
  6.3 0.9 %copy-done.5 = bf16[256,256]{1,0:T(8,128)(2,1)S(1)} copy-done((bf16[256,256]{1,0:T(8,128)(2,1)S(1)}, bf16[256,256]{1,0:T(8,128)(2,1)}, u32[]{:S(2)}) %copy-start.5) | copy-done | bytes 131096
  7.2 0.0 copy-start.6
  7.2 0.7 copy-done.6
  7.9 68.3 %shard_map.155 = (bf16[64,1024]{1,0:T(8,128)(2,1)S(1)}, bf16[64,1024]{1,0:T(8,128)(2,1)S(1)}, f32[64,256]{1,0:T(8,128)S(1)}, f32[64,256]{1,0:T(8,128)S(1)}, f32[1,64]{1,0:T(1,128)S(1)}) custom-call(s32[2,12]{1,0:T(2,128)S(1)} %bitcast.23, s32[4,7]{1,0:T(4,128)S(1)} %bitcast.21, s32[4,7]{1,0:T(4,128)S(1)} %bitcast.22, s32[1,7]{1,0:T(1,128)S(1)} %copy-done.11, ...), custom_call_target="tpu_custom_call" | custom-call | tf_op jit(solution)/shard_map/pallas_call | solution.py:344
  76.2 0.7 copy.22
  76.9 0.7 copy.23
  77.5 0.6 copy.24
  78.2 0.6 copy.25
  78.8 0.5 copy.26
Async XLA Ops:
  0.6 0.7 copy-start.10
  0.6 0.7 copy-start.8
  0.7 0.7 copy-start.7
  0.7 0.7 copy-start.9
  0.7 0.7 copy-start.11
  1.4 1.2 %copy-start = (bf16[1,7,4,128,128]{4,3,2,1,0:T(8,128)(2,1)S(1)}, bf16[1,7,4,128,128]{4,3,2,1,0:T(8,128)(2,1)}, u32[]{:S(2)}) copy-start(bf16[1,7,4,128,128]{4,3,2,1,0:T(8,128)(2,1)} %param.23) | copy-start | bytes 2752516
  2.5 1.0 %copy-start.1 = (bf16[1,12,128,128]{3,2,1,0:T(8,128)(2,1)S(1)}, bf16[1,12,128,128]{3,2,1,0:T(8,128)(2,1)}, u32[]{:S(2)}) copy-start(bf16[1,12,128,128]{3,2,1,0:T(8,128)(2,1)} %param.18) | copy-start | bytes 1179652
  3.5 0.9 %copy-start.2 = (bf16[64,1024]{1,0:T(8,128)(2,1)S(1)}, bf16[64,1024]{1,0:T(8,128)(2,1)}, u32[]{:S(2)}) copy-start(bf16[64,1024]{1,0:T(8,128)(2,1)} %feat.1) | copy-start | bytes 393220
  4.4 0.9 %copy-start.3 = (bf16[64,1024]{1,0:T(8,128)(2,1)S(1)}, bf16[64,1024]{1,0:T(8,128)(2,1)}, u32[]{:S(2)}) copy-start(bf16[64,1024]{1,0:T(8,128)(2,1)} %cot.1) | copy-start | bytes 393220
  5.4 0.9 %copy-start.4 = (bf16[256,256]{1,0:T(8,128)(2,1)S(1)}, bf16[256,256]{1,0:T(8,128)(2,1)}, u32[]{:S(2)}) copy-start(bf16[256,256]{1,0:T(8,128)(2,1)} %w_self.1) | copy-start | bytes 393220
  6.3 0.9 %copy-start.5 = (bf16[256,256]{1,0:T(8,128)(2,1)S(1)}, bf16[256,256]{1,0:T(8,128)(2,1)}, u32[]{:S(2)}) copy-start(bf16[256,256]{1,0:T(8,128)(2,1)} %w_neigh.1) | copy-start | bytes 393220
  7.2 0.7 copy-start.6

commit v2 on v1

--- a/solution.py
+++ b/solution.py
@@ -22,6 +22,7 @@
 GROUP = 2 * XS
 SEND_ORDER = (4, 3, 2, 6, 1, 5, 0)
 TAKE_ORDER = (0, 5, 1, 6, 2, 3, 4)
+LIMIT = 60 * 1024 * 1024
 N_COPIES = 2 * LEVELS + 7 * (YS - 1) + 2 * (GROUP - 1) + 9
 
 
@@ -35,13 +36,34 @@
 
 def kernel(
     scale,
-    pairs, cdst, csrc, ccnt,
-    feat, cot, w_self, w_neigh, bias, bound, ltile, ctile,
+    pairs_in, cdst_in, csrc_in, ccnt_in, feat_in, cot_in, w_self_in, w_neigh_in, bias_in, bound_in, ltile_in, ctile_in,
+    out_hbm, gfeat_hbm, gself_hbm, gneigh_hbm, gbias_hbm,
     out, gfeat, gself, gneigh, gbias,
+    pairs, cdst, csrc, ccnt, feat, cot, w_self, w_neigh, bias, bound, ltile, ctile,
     onehot, fb, cb, xs, xr0, xr1, xr2, xr3, xr4, xr5, xr6, bs, br, acc, gacc, fa, cot3, agg, wp, wpt, bcol,
     sl3, o3, outr, du, upr, dnr, gf, gs, gr, cs, cr, zs, zr, us, ur, pg, full,
-    send, recv,
+    send, recv, fetch, ship,
 ):
+    fetched = {}
+    for n, (name, src, dst) in enumerate((
+        ("bound", bound_in, bound), ("feat", feat_in, feat), ("cot", cot_in, cot),
+        ("pairs", pairs_in, pairs), ("ltile", ltile_in, ltile),
+        ("csrc", csrc_in, csrc), ("cdst", cdst_in, cdst), ("ccnt", ccnt_in, ccnt), ("ctile", ctile_in, ctile),
+        ("w_self", w_self_in, w_self), ("w_neigh", w_neigh_in, w_neigh), ("bias", bias_in, bias),
+    )):
+        fetched[name] = pltpu.make_async_copy(src, dst, fetch.at[n])
+        fetched[name].start()
+
+    shipped = []
+
+    def give(n, src, dst):
+        shipped.append(pltpu.make_async_copy(src, dst, ship.at[n]))
+        shipped[-1].start()
+
+    def need(*names):
+        for name in names:
+            fetched[name].wait()
+
     xr = (xr0, xr1, xr2, xr3, xr4, xr5, xr6)
     y = lax.axis_index("feat")
     o = lax.axis_index("dom")
@@ -97,8 +119,11 @@
     def rows(start, size):
         return pl.ds(pl.multiple_of(start, size), size)
 
+    need("bound", "feat")
     for b in range(NB):
         fb[b] = feat[:, b * BLK:(b + 1) * BLK]
+    need("cot")
+    for b in range(NB):
         cb[b] = cot[:, b * BLK:(b + 1) * BLK]
 
     def gather(level):
@@ -148,6 +173,7 @@
 
         lax.fori_loop(0, NB, one, 0)
 
+    need("pairs", "ltile")
     acc[...] = jnp.zeros_like(acc)
     for first in range(0, NLT, 4):
         tiles = range(first, first + 4)
@@ -157,6 +183,7 @@
             [jnp.float32(1.0)] * 4,
         )
 
+    need("w_self", "w_neigh", "bias")
     row = lax.broadcasted_iota(jnp.int32, (512, 256), 0)
     col = lax.broadcasted_iota(jnp.int32, (512, 256), 1)
     spot = (col >> 6) * 128 + (col & 63)
@@ -172,6 +199,7 @@
     def live_of(level, slot):
         return jnp.where(slot < ccnt[0, level], 1.0, 0.0)
 
+    need("csrc", "cdst", "ccnt", "ctile")
     for level in TAKE_ORDER:
         forward[level].wait_recv()
         place(
@@ -298,6 +326,7 @@
     tile = (us[...] + ur[0] + ur[1] + ur[2]) * scale
     pg[zl] = tile[0:8]
     gbias[...] = tile[8:9, 0:64]
+    give(4, gbias, gbias_hbm)
     grad_waits = [push(pg.at[zl], pg.at[zl], pg.at[zl_from[k]], zl_dev[k]) for k in range(1, 4)]
 
     take_back(TAKE_ORDER[2])
@@ -312,12 +341,10 @@
     for b in range(NB):
         out[:, b * BLK:(b + 1) * BLK] = outr[b]
         acc[b] = acc[b] + dnr[b].astype(F32)
-
-    for level in TAKE_ORDER[3:]:
+    give(0, out, out_hbm)
+
+    for level in TAKE_ORDER[3:-1]:
         take_back(level)
-    for b in range(NB):
-        lanes = slice(b * BLK, (b + 1) * BLK)
-        gfeat[:, lanes] = (gacc[:, lanes] + acc[b]).astype(BF16)
 
     for wait in grad_waits:
         wait.wait_recv()
@@ -328,9 +355,32 @@
             for p in range(4):
                 first = (k % 2) * 32 + p * 8
                 dst[first:first + 8, lanes] = full[half * 4 + k, p]
+    give(2, gself, gself_hbm)
+    give(3, gneigh, gneigh_hbm)
+
+    take_back(TAKE_ORDER[-1])
+    for b in range(NB):
+        lanes = slice(b * BLK, (b + 1) * BLK)
+        gfeat[:, lanes] = (gacc[:, lanes] + acc[b]).astype(BF16)
+    give(1, gfeat, gfeat_hbm)
 
     for copy in sent:
         copy.wait_send()
+    for copy in shipped:
+        copy.wait()
+
+
+def deliver(*refs):
+    (load, store), held = refs[-2:], refs[10:15]
+    loads = [pltpu.make_async_copy(refs[n], held[n], load.at[n]) for n in range(5)]
+    stores = [pltpu.make_async_copy(held[n], refs[5 + n], store.at[n]) for n in range(5)]
+    for copy in loads:
+        copy.start()
+    for before, after in zip(loads, stores):
+        before.wait()
+        after.start()
+    for copy in stores:
+        copy.wait()
 
 
 def on_device(
@@ -338,21 +388,34 @@
     boundary, cross_dst, cross_src, cross_count, cross_tiles,
 ):
     nodes = features.shape[1] * lax.axis_size("dom")
-    vmem = pl.BlockSpec(memory_space=pltpu.VMEM)
-    smem = pl.BlockSpec(memory_space=pltpu.SMEM)
+    anywhere = pl.BlockSpec(memory_space=pl.ANY)
+    shapes = (
+        jax.ShapeDtypeStruct((FL, NB * BLK), BF16),
+        jax.ShapeDtypeStruct((FL, NB * BLK), BF16),
+        jax.ShapeDtypeStruct((FL, 256), F32),
+        jax.ShapeDtypeStruct((FL, 256), F32),
+        jax.ShapeDtypeStruct((1, FL), F32),
+    )
     blocks = (NB, FL, BLK)
     results = pl.pallas_call(
         functools.partial(kernel, 1.0 / math.sqrt(nodes)),
-        out_shape=(
-            jax.ShapeDtypeStruct((FL, NB * BLK), BF16),
-            jax.ShapeDtypeStruct((FL, NB * BLK), BF16),
-            jax.ShapeDtypeStruct((FL, 256), F32),
-            jax.ShapeDtypeStruct((FL, 256), F32),
-            jax.ShapeDtypeStruct((1, FL), F32),
-        ),
-        in_specs=[smem] * 4 + [vmem] * 8,
-        out_specs=(vmem,) * 5,
+        out_shape=shapes,
+        in_specs=[anywhere] * 12,
+        out_specs=(anywhere,) * 5,
         scratch_shapes=[
+            *[pltpu.VMEM(one.shape, one.dtype) for one in shapes],
+            pltpu.SMEM((2, NLT), jnp.int32),
+            pltpu.SMEM((CT, LEVELS), jnp.int32),
+            pltpu.SMEM((CT, LEVELS), jnp.int32),
+            pltpu.SMEM((1, LEVELS), jnp.int32),
+            pltpu.VMEM((FL, NB * BLK), BF16),
+            pltpu.VMEM((FL, NB * BLK), BF16),
+            pltpu.VMEM((256, 256), BF16),
+            pltpu.VMEM((256, 256), BF16),
+            pltpu.VMEM((1, 256), F32),
+            pltpu.VMEM((LEVELS, 1, CT * BLK), jnp.int32),
+            pltpu.VMEM((NLT, BLK, BLK), BF16),
+            pltpu.VMEM((LEVELS * CT, BLK, BLK), BF16),
             pltpu.VMEM((LEVELS, NB * BLK, CT * BLK), BF16),
             pltpu.VMEM(blocks, BF16),
             pltpu.VMEM(blocks, BF16),
@@ -387,9 +450,11 @@
             pltpu.VMEM((GROUP, 4, 8, BLK), F32),
             pltpu.SemaphoreType.DMA((N_COPIES,)),
             pltpu.SemaphoreType.DMA((N_COPIES,)),
+            pltpu.SemaphoreType.DMA((12,)),
+            pltpu.SemaphoreType.DMA((5,)),
         ],
         compiler_params=pltpu.CompilerParams(
-            collective_id=0, has_side_effects=True, vmem_limit_bytes=40 * 1024 * 1024
+            collective_id=0, has_side_effects=True, vmem_limit_bytes=LIMIT
         ),
     )(
         local_pairs[0].T,
@@ -405,7 +470,17 @@
         local_tiles[0],
         cross_tiles.reshape(LEVELS * CT, BLK, BLK),
     )
-    out, gfeat, gself, gneigh, gbias = results
+    out, gfeat, gself, gneigh, gbias = pl.pallas_call(
+        deliver,
+        out_shape=shapes,
+        in_specs=[anywhere] * 5,
+        out_specs=(anywhere,) * 5,
+        scratch_shapes=[
+            *[pltpu.VMEM(one.shape, one.dtype) for one in shapes],
+            pltpu.SemaphoreType.DMA((5,)),
+            pltpu.SemaphoreType.DMA((5,)),
+        ],
+    )(*results)
     return out, gfeat, gself.T, gneigh.T, gbias.reshape(FL)
 
 

time: 79.6 us -> 71.5 us (0.90)
  local copies, waits for them, and re-layouts: 10.3 us -> 0 us
  Pallas kernels: 68.3 us -> 70.7 us
    unnamed x29 -> x0, local copies, waits for them, and re-layouts: 10.3 us -> none
    pallas_call x0 -> x1, Pallas kernels: none -> 1.75 us  [on_device(): pl.pallas_call(deliver, out_shape=shapes, in_specs=[anywhere] * 5, out_sp...]
where the time goes in v2:
time: 71.5 us; the launch traced here: 71.3 us
  Pallas kernels  70.7 us (99%)
    pallas_call x1, Pallas kernels, on_device(): pl.pallas_call(functools.partial(kernel, 1.0 / math.sqrt(nodes)), out_sha...  68.9 us
    pallas_call x1, Pallas kernels, on_device(): pl.pallas_call(deliver, out_shape=shapes, in_specs=[anywhere] * 5, out_sp...  1.75 us

profile of v2, /device:TPU:1, one launch (start us, length us, event | category | flops | bytes accessed | tf_op | source)
XLA Modules:
  0.0 71.3 jit_solution(13049020915616279554)
XLA Ops:
  0.6 68.9 %shard_map.155 = (bf16[64,1024]{1,0:T(8,128)(2,1)}, bf16[64,1024]{1,0:T(8,128)(2,1)}, f32[64,256]{1,0:T(8,128)}, f32[64,256]{1,0:T(8,128)}, f32[1,64]{1,0:T(1,128)}) custom-call(s32[2,12]{1,0:T(2,128)} %bitcast.21, s32[4,7]{1,0:T(4,128)} %bitcast.19, s32[4,7]{1,0:T(4,128)} %bitcast.20, s32[1,7]{1,0:T(1,128)} %ccnt_in.1, bf16[64,1024]{1,0:T(8,128)(2,1)} %feat_in.1, ...), custom_call_target="tpu_custom_call" | custom-call | tf_op jit(solution)/shard_map/pallas_call | solution.py:400
  69.5 1.8 %shard_map.156 = (bf16[64,1024]{1,0:T(8,128)(2,1)}, bf16[64,1024]{1,0:T(8,128)(2,1)}, f32[64,256]{1,0:T(8,128)}, f32[64,256]{1,0:T(8,128)}, f32[1,64]{1,0:T(1,128)}) custom-call(bf16[64,1024]{1,0:T(8,128)(2,1)} %get-tuple-element.15.refs_0_, bf16[64,1024]{1,0:T(8,128)(2,1)} %get-tuple-element.16.refs_1_, f32[64,256]{1,0:T(8,128)} %get-tuple-element.17.refs_2_, ...), custom_call_target="tpu_custom_call" | custom-call | tf_op jit(solution)/shard_map/pallas_call | solution.py:473

commit v3 on v2

--- a/solution.py
+++ b/solution.py
@@ -19,11 +19,11 @@
 LEVELS = 7
 XS, ZS, YS = 4, 16, 4
 FL = 64
-GROUP = 2 * XS
 SEND_ORDER = (4, 3, 2, 6, 1, 5, 0)
+HELD = (3, 2, 1)
 TAKE_ORDER = (0, 5, 1, 6, 2, 3, 4)
 LIMIT = 60 * 1024 * 1024
-N_COPIES = 2 * LEVELS + 7 * (YS - 1) + 2 * (GROUP - 1) + 9
+N_COPIES = 2 * LEVELS + 6 * (YS - 1) + 2 * (YS * XS - 1) + ZS - 1 + 3
 
 
 def nt(a, b):
@@ -41,7 +41,7 @@
     out, gfeat, gself, gneigh, gbias,
     pairs, cdst, csrc, ccnt, feat, cot, w_self, w_neigh, bias, bound, ltile, ctile,
     onehot, fb, cb, xs, xr0, xr1, xr2, xr3, xr4, xr5, xr6, bs, br, acc, gacc, fa, cot3, agg, wp, wpt, bcol,
-    sl3, o3, outr, du, upr, dnr, gf, gs, gr, cs, cr, zs, zr, us, ur, pg, full,
+    sl3, o3, outr, du, upr, dnr, gt, gc, gsum, gb, gbc, gbs, gs, gr, us, zs, zr, full, fullc,
     send, recv, fetch, ship,
 ):
     fetched = {}
@@ -71,11 +71,9 @@
     z = lax.rem(lax.div(o, 2), ZS)
     x = lax.div(o, 2 * ZS)
     zl = lax.rem(z, 4)
-    zh = lax.div(z, 4)
-    g = x * 2 + core
-
-    def at(g_, z_):
-        return lax.div(g_, 2) * (2 * ZS) + z_ * 2 + lax.rem(g_, 2)
+
+    def at(x_, z_):
+        return x_ * (2 * ZS) + z_ * 2 + core
 
     def partner(level):
         step = 1 << level
@@ -83,19 +81,28 @@
 
     y_to = [lax.rem(y + k, YS) for k in range(YS)]
     y_from = [lax.rem(y + YS - k, YS) for k in range(YS)]
-    g_to = [lax.rem(g + k, GROUP) for k in range(GROUP)]
-    g_from = [lax.rem(g + GROUP - k, GROUP) for k in range(GROUP)]
-    zl_to = [lax.rem(zl + k, 4) for k in range(4)]
-    zl_from = [lax.rem(zl + 4 - k, 4) for k in range(4)]
-    zh_to = [lax.rem(zh + k, 4) for k in range(4)]
-
+    x_to = [lax.rem(x + k, XS) for k in range(XS)]
+    x_from = [lax.rem(x + XS - k, XS) for k in range(XS)]
+    def z_off(k):
+        return lax.rem(z + ZS + k, ZS)
+
+    def z_off(k):
+        return lax.rem(z + ZS + k, ZS)
+
+    far_z = sorted(range(1, ZS), key=lambda k: -min(k, ZS - k))
     y_dev = [{"feat": y_to[k]} for k in range(YS)]
-    g_dev = [{"dom": at(g_to[k], z)} for k in range(GROUP)]
-    zl_dev = [{"dom": at(g, zh * 4 + zl_to[k])} for k in range(4)]
-    zh_dev = [{"dom": at(g, zh_to[k] * 4 + zl)} for k in range(4)]
+    z_dev = {k: {"dom": at(x, z_off(k))} for k in far_z}
+    plane = sorted(
+        ((k, q) for k in range(XS) for q in range(YS) if k or q),
+        key=lambda kq: -sum(min(k, 4 - k) for k in kq),
+    )
+    plane_dev = [{"dom": at(x_to[k], z), "feat": y_to[q]} for k, q in plane]
+    near = [(k, d) for k in (2, 1, 3, 0) for d in (2, 1, -1, 0) if k or d]
+    other_core = {"dom": o + 1 - 2 * core}
 
     barrier = pltpu.get_barrier_semaphore()
-    greeted = y_dev[1:] + g_dev[1:] + zl_dev[1:] + zh_dev[1:]
+    greeted = [other_core] + plane_dev + list(z_dev.values())
+    greeted += [{"dom": at(x_from[k], z_off(-d))} for k, d in near if k and d]
     for dev in greeted:
         pl.semaphore_signal(barrier, inc=1, device_id=dev, device_id_type=MESH)
 
@@ -143,7 +150,28 @@
     def send_level(level, src, dst):
         return push(src, dst, dst, {"dom": partner(level)})
 
-    gather(SEND_ORDER[0])
+    for level in SEND_ORDER:
+        gather(level)
+    def place(products, targets, lives):
+        def one(b, carry):
+            total = acc[b]
+            for product, target, live in zip(products, targets, lives):
+                total = total + product * jnp.where(target == b, live, 0.0)
+            acc[b] = total
+            return carry
+
+        lax.fori_loop(0, NB, one, 0)
+
+    need("pairs", "ltile")
+    acc[...] = jnp.zeros_like(acc)
+    for first in range(0, NLT, 4):
+        tiles = range(first, first + 4)
+        place(
+            [nt(fb[pairs[1, t]], ltile[t]) for t in tiles],
+            [pairs[0, t] for t in tiles],
+            [jnp.float32(1.0)] * 4,
+        )
+
     pl.semaphore_wait(barrier, len(greeted))
 
     forward = {SEND_ORDER[0]: send_level(SEND_ORDER[0], xs.at[SEND_ORDER[0]], xr[SEND_ORDER[0]])}
@@ -156,32 +184,11 @@
             cb.at[pl.ds(2 * y_to[k], 2)], cot3.at[:, rows(y * 64, 64), :],
             cot3.at[:, rows(y_from[k] * 64, 64), :], y_dev[k]))
     for level in SEND_ORDER[1:]:
-        gather(level)
         forward[level] = send_level(level, xs.at[level], xr[level])
 
     for b in range(2):
         fa[b, rows(y * 128, 64), :] = fb[2 * y + b]
         cot3[b, rows(y * 64, 64), :] = cb[2 * y + b]
-
-    def place(products, targets, lives):
-        def one(b, carry):
-            total = acc[b]
-            for product, target, live in zip(products, targets, lives):
-                total = total + product * jnp.where(target == b, live, 0.0)
-            acc[b] = total
-            return carry
-
-        lax.fori_loop(0, NB, one, 0)
-
-    need("pairs", "ltile")
-    acc[...] = jnp.zeros_like(acc)
-    for first in range(0, NLT, 4):
-        tiles = range(first, first + 4)
-        place(
-            [nt(fb[pairs[1, t]], ltile[t]) for t in tiles],
-            [pairs[0, t] for t in tiles],
-            [jnp.float32(1.0)] * 4,
-        )
 
     need("w_self", "w_neigh", "bias")
     row = lax.broadcasted_iota(jnp.int32, (512, 256), 0)
@@ -234,20 +241,31 @@
             du.at[:, rows(y_to[k] * 128 + 64, 64), :], upr.at[pl.ds(2 * y, 2)],
             upr.at[pl.ds(2 * y_from[k], 2)], y_dev[k]))
 
-    for half in range(2):
-        total = sum(nt(fa[b], sl3[b, half * 128:(half + 1) * 128, :]) for b in range(2))
-        for k in range(YS):
-            gf[k, half * 128:(half + 1) * 128, :] = total[k * 128:(k + 1) * 128]
-    ones = jnp.ones((16, 128), BF16)
+    def grads_of(half):
+        return sum(nt(fa[b], sl3[b, rows(half * 128, 128), :]) for b in range(2))
+
+    gt[...] = grads_of(1 - core)
+    core_waits = [push(gt, gc, gc, other_core)]
+    ones = jnp.ones((8, 128), BF16)
     blank = jnp.zeros((64, 128), BF16)
     for k in range(YS):
-        gf[k, 256:272, :] = sum(
+        gb[k] = sum(
             nt(ones, jnp.concatenate([sl3[b, k * 64:(k + 1) * 64, :], blank], axis=0)) for b in range(2)
         )
-    gs[...] = gf[...].astype(BF16)
+    core_waits.append(push(gb, gbc, gbc, other_core))
+    gsum[...] = grads_of(core)
+    for wait in core_waits:
+        wait.wait_recv()
+    gsum[...] += gc[...]
+    for k in range(YS):
+        gbs[k] = gb[k] + gbc[k]
+        for i in range(XS):
+            first = k * 128 + i * 32
+            gs[k, i, 0:32, :] = gsum[first:first + 32, :].astype(BF16)
+            gs[k, i, 32:48, :] = jnp.concatenate([gbs[k], gbs[k]], axis=0).astype(BF16)
     grad_waits = []
-    for k in range(1, YS):
-        grad_waits.append(push(gs.at[y_to[k]], gr.at[k - 1], gr.at[k - 1], y_dev[k]))
+    for n, (k, q) in enumerate(plane):
+        grad_waits.append(push(gs.at[y_to[q], x_to[k]], gr.at[n], gr.at[n], plane_dev[n]))
 
     for b in range(2):
         upr[2 * y + b] = du[b, rows(y * 128 + 64, 64), :]
@@ -262,6 +280,33 @@
                 slot = jnp.where(csrc[c, level] == k, c, slot)
             term = nn(upr[cdst[slot, level]], ctile[level * CT + slot])
             bs[level, k] = (term * live_of(level, slot)).astype(BF16)
+        if level not in HELD:
+            backward[level] = send_level(level, bs.at[level], br.at[level])
+
+    acc[...] = jnp.zeros_like(acc)
+    for first in range(0, NLT, 4):
+        tiles = range(first, first + 4)
+        place(
+            [nn(upr[pairs[0, t]], ltile[t]) for t in tiles],
+            [pairs[1, t] for t in tiles],
+            [jnp.float32(1.0)] * 4,
+        )
+
+    for wait in grad_waits:
+        wait.wait_recv()
+    part = gsum[rows(y * 128 + x * 32, 32), :]
+    bias_part = gbs[y]
+    for n in range(len(plane)):
+        part = part + gr[n, 0:32, :].astype(F32)
+        bias_part = bias_part + gr[n, 32:48, :].astype(F32)[0:8]
+    for k in range(4):
+        piece = jnp.concatenate([part[k * 8:(k + 1) * 8], bias_part], axis=0)
+        us[k] = piece
+        zs[k] = piece.astype(BF16)
+    grad_waits = [
+        push(zs.at[lax.rem(zl + k, 4)], zr.at[k - 1], zr.at[k - 1], z_dev[k]) for k in far_z
+    ]
+    for level in HELD:
         backward[level] = send_level(level, bs.at[level], br.at[level])
 
     for k in range(1, YS):
@@ -275,66 +320,29 @@
         outr[2 * y + b] = o3[b, rows(y * 64, 64), :]
         dnr[2 * y + b] = du[b, rows(y * 128, 64), :]
 
-    for wait in grad_waits:
-        wait.wait_recv()
-    part = gf[y]
-    for k in range(YS - 1):
-        part = part + gr[k].astype(F32)
-    for k in range(GROUP):
-        cs[k, 0:32, :] = part[k * 32:(k + 1) * 32]
-        cs[k, 32:40, :] = part[256:264]
-    grad_waits = [
-        push(cs.at[g_to[k]], cr.at[k - 1], cr.at[k - 1], g_dev[k]) for k in range(1, GROUP)
-    ]
-
-    acc[...] = jnp.zeros_like(acc)
-    for first in range(0, NLT, 4):
-        tiles = range(first, first + 4)
-        place(
-            [nn(upr[pairs[0, t]], ltile[t]) for t in tiles],
-            [pairs[1, t] for t in tiles],
-            [jnp.float32(1.0)] * 4,
-        )
-
-    for wait in grad_waits:
-        wait.wait_recv()
-    part = cs[g]
-    for k in range(GROUP - 1):
-        part = part + cr[k]
-    for k in range(4):
-        zs[k, 0:8, :] = part[k * 8:(k + 1) * 8]
-        zs[k, 8:16, :] = part[32:40]
-    grad_waits = [push(zs.at[zl_to[k]], zr.at[k - 1], zr.at[k - 1], zl_dev[k]) for k in range(1, 4)]
-
     def take_back(level):
         backward[level].wait_recv()
         terms = jnp.concatenate([br[level, k] for k in range(CT)], axis=1)
         gacc[...] += nt(terms, onehot[level])
 
     gacc[...] = jnp.zeros_like(gacc)
-    take_back(TAKE_ORDER[0])
+    for level in (0, 5, 6):
+        take_back(level)
 
     for wait in grad_waits:
         wait.wait_recv()
-    us[...] = zs[zl] + zr[0] + zr[1] + zr[2]
-    grad_waits = [push(us, ur.at[k - 1], ur.at[k - 1], zh_dev[k]) for k in range(1, 4)]
-
-    take_back(TAKE_ORDER[1])
-
-    for wait in grad_waits:
-        wait.wait_recv()
-    tile = (us[...] + ur[0] + ur[1] + ur[2]) * scale
-    pg[zl] = tile[0:8]
+    tile = us[zl]
+    for n in range(ZS - 1):
+        tile = tile + zr[n].astype(F32)
+    tile = tile * scale
+    full[x, zl] = tile[0:8]
+    grad_waits = [
+        push(full.at[x, zl], full.at[x, zl], full.at[x_from[k], lax.rem(zl + 4 - d, 4)],
+             {"dom": at(x_to[k], z_off(d))})
+        for k, d in near
+    ]
     gbias[...] = tile[8:9, 0:64]
     give(4, gbias, gbias_hbm)
-    grad_waits = [push(pg.at[zl], pg.at[zl], pg.at[zl_from[k]], zl_dev[k]) for k in range(1, 4)]
-
-    take_back(TAKE_ORDER[2])
-
-    for wait in grad_waits:
-        wait.wait_recv()
-    full[g] = pg[...]
-    grad_waits = [push(full.at[g], full.at[g], full.at[g_from[k]], g_dev[k]) for k in range(1, GROUP)]
 
     for wait in late:
         wait.wait_recv()
@@ -343,22 +351,28 @@
         acc[b] = acc[b] + dnr[b].astype(F32)
     give(0, out, out_hbm)
 
-    for level in TAKE_ORDER[3:-1]:
+    for level in (1, 2, 3):
         take_back(level)
 
     for wait in grad_waits:
         wait.wait_recv()
-    for half in range(2):
-        for k in range(4):
-            lanes = slice(half * 128, (half + 1) * 128)
+    half_wait = push(full, fullc, fullc, other_core)
+
+    def assemble(tiles, half):
+        lanes = rows(half * 128, 128)
+        for k in range(XS):
             dst = gself if k < 2 else gneigh
             for p in range(4):
                 first = (k % 2) * 32 + p * 8
-                dst[first:first + 8, lanes] = full[half * 4 + k, p]
+                dst[first:first + 8, lanes] = tiles[k, p]
+
+    assemble(full, core)
+    half_wait.wait_recv()
+    assemble(fullc, 1 - core)
     give(2, gself, gself_hbm)
     give(3, gneigh, gneigh_hbm)
 
-    take_back(TAKE_ORDER[-1])
+    take_back(4)
     for b in range(NB):
         lanes = slice(b * BLK, (b + 1) * BLK)
         gfeat[:, lanes] = (gacc[:, lanes] + acc[b]).astype(BF16)
@@ -437,17 +451,18 @@
             pltpu.VMEM((2, 512, BLK), BF16),
             pltpu.VMEM(blocks, BF16),
             pltpu.VMEM(blocks, BF16),
-            pltpu.VMEM((YS, 272, BLK), F32),
-            pltpu.VMEM((YS, 272, BLK), BF16),
-            pltpu.VMEM((YS - 1, 272, BLK), BF16),
-            pltpu.VMEM((GROUP, 40, BLK), F32),
-            pltpu.VMEM((GROUP - 1, 40, BLK), F32),
+            pltpu.VMEM((512, BLK), F32),
+            pltpu.VMEM((512, BLK), F32),
+            pltpu.VMEM((512, BLK), F32),
+            pltpu.VMEM((YS, 8, BLK), F32),
+            pltpu.VMEM((YS, 8, BLK), F32),
+            pltpu.VMEM((YS, 8, BLK), F32),
+            pltpu.VMEM((YS, XS, 48, BLK), BF16),
+            pltpu.VMEM((YS * XS - 1, 48, BLK), BF16),
             pltpu.VMEM((4, 16, BLK), F32),
-            pltpu.VMEM((3, 16, BLK), F32),
-            pltpu.VMEM((16, BLK), F32),
-            pltpu.VMEM((3, 16, BLK), F32),
-            pltpu.VMEM((4, 8, BLK), F32),
-            pltpu.VMEM((GROUP, 4, 8, BLK), F32),
+            pltpu.VMEM((4, 16, BLK), BF16),
+            pltpu.VMEM((ZS - 1, 16, BLK), BF16),
+            *[pltpu.VMEM((XS, 4, 8, BLK), F32)] * 2,
             pltpu.SemaphoreType.DMA((N_COPIES,)),
             pltpu.SemaphoreType.DMA((N_COPIES,)),
             pltpu.SemaphoreType.DMA((12,)),

time: 71.5 us -> 67.7 us (0.947)
  Pallas kernels: 70.7 us -> 66.9 us
    pallas_call x1, Pallas kernels: 68.9 us -> 65.1 us  [on_device(): pl.pallas_call(functools.partial(kernel, 1.0 / math.sqrt(nodes)), out_sha...]
where the time goes in v3:
time: 67.7 us; the launch traced here: 67.5 us
  Pallas kernels  66.9 us (99%)
    pallas_call x1, Pallas kernels, on_device(): pl.pallas_call(functools.partial(kernel, 1.0 / math.sqrt(nodes)), out_sha...  65.1 us
    pallas_call x1, Pallas kernels, on_device(): pl.pallas_call(deliver, out_shape=shapes, in_specs=[anywhere] * 5, out_sp...  1.75 us

profile of v3, /device:TPU:1, one launch (start us, length us, event | category | flops | bytes accessed | tf_op | source)
XLA Modules:
  0.0 67.5 jit_solution(943882941404606339)
XLA Ops:
  0.6 65.1 %shard_map.155 = (bf16[64,1024]{1,0:T(8,128)(2,1)}, bf16[64,1024]{1,0:T(8,128)(2,1)}, f32[64,256]{1,0:T(8,128)}, f32[64,256]{1,0:T(8,128)}, f32[1,64]{1,0:T(1,128)}) custom-call(s32[2,12]{1,0:T(2,128)} %bitcast.21, s32[4,7]{1,0:T(4,128)} %bitcast.19, s32[4,7]{1,0:T(4,128)} %bitcast.20, s32[1,7]{1,0:T(1,128)} %ccnt_in.1, bf16[64,1024]{1,0:T(8,128)(2,1)} %feat_in.1, ...), custom_call_target="tpu_custom_call" | custom-call | tf_op jit(solution)/shard_map/pallas_call | solution.py:414
  65.8 1.8 %shard_map.156 = (bf16[64,1024]{1,0:T(8,128)(2,1)}, bf16[64,1024]{1,0:T(8,128)(2,1)}, f32[64,256]{1,0:T(8,128)}, f32[64,256]{1,0:T(8,128)}, f32[1,64]{1,0:T(1,128)}) custom-call(bf16[64,1024]{1,0:T(8,128)(2,1)} %get-tuple-element.15.refs_0_, bf16[64,1024]{1,0:T(8,128)(2,1)} %get-tuple-element.16.refs_1_, f32[64,256]{1,0:T(8,128)} %get-tuple-element.17.refs_2_, ...), custom_call_target="tpu_custom_call" | custom-call | tf_op jit(solution)/shard_map/pallas_call | solution.py:488

commit v4 on v3

--- a/solution.py
+++ b/solution.py
@@ -44,26 +44,6 @@
     sl3, o3, outr, du, upr, dnr, gt, gc, gsum, gb, gbc, gbs, gs, gr, us, zs, zr, full, fullc,
     send, recv, fetch, ship,
 ):
-    fetched = {}
-    for n, (name, src, dst) in enumerate((
-        ("bound", bound_in, bound), ("feat", feat_in, feat), ("cot", cot_in, cot),
-        ("pairs", pairs_in, pairs), ("ltile", ltile_in, ltile),
-        ("csrc", csrc_in, csrc), ("cdst", cdst_in, cdst), ("ccnt", ccnt_in, ccnt), ("ctile", ctile_in, ctile),
-        ("w_self", w_self_in, w_self), ("w_neigh", w_neigh_in, w_neigh), ("bias", bias_in, bias),
-    )):
-        fetched[name] = pltpu.make_async_copy(src, dst, fetch.at[n])
-        fetched[name].start()
-
-    shipped = []
-
-    def give(n, src, dst):
-        shipped.append(pltpu.make_async_copy(src, dst, ship.at[n]))
-        shipped[-1].start()
-
-    def need(*names):
-        for name in names:
-            fetched[name].wait()
-
     xr = (xr0, xr1, xr2, xr3, xr4, xr5, xr6)
     y = lax.axis_index("feat")
     o = lax.axis_index("dom")
@@ -83,9 +63,6 @@
     y_from = [lax.rem(y + YS - k, YS) for k in range(YS)]
     x_to = [lax.rem(x + k, XS) for k in range(XS)]
     x_from = [lax.rem(x + XS - k, XS) for k in range(XS)]
-    def z_off(k):
-        return lax.rem(z + ZS + k, ZS)
-
     def z_off(k):
         return lax.rem(z + ZS + k, ZS)
 
@@ -101,10 +78,30 @@
     other_core = {"dom": o + 1 - 2 * core}
 
     barrier = pltpu.get_barrier_semaphore()
-    greeted = [other_core] + plane_dev + list(z_dev.values())
+    greeted = list(z_dev.values()) + [other_core] + plane_dev
     greeted += [{"dom": at(x_from[k], z_off(-d))} for k, d in near if k and d]
     for dev in greeted:
         pl.semaphore_signal(barrier, inc=1, device_id=dev, device_id_type=MESH)
+
+    fetched = {}
+    for n, (name, src, dst) in enumerate((
+        ("bound", bound_in, bound), ("feat", feat_in, feat), ("cot", cot_in, cot),
+        ("pairs", pairs_in, pairs), ("ltile", ltile_in, ltile),
+        ("csrc", csrc_in, csrc), ("cdst", cdst_in, cdst), ("ccnt", ccnt_in, ccnt), ("ctile", ctile_in, ctile),
+        ("w_self", w_self_in, w_self), ("w_neigh", w_neigh_in, w_neigh), ("bias", bias_in, bias),
+    )):
+        fetched[name] = pltpu.make_async_copy(src, dst, fetch.at[n])
+        fetched[name].start()
+
+    shipped = []
+
+    def give(n, src, dst):
+        shipped.append(pltpu.make_async_copy(src, dst, ship.at[n]))
+        shipped[-1].start()
+
+    def need(*names):
+        for name in names:
+            fetched[name].wait()
 
     counter = [0]
     sent = []
@@ -152,6 +149,7 @@
 
     for level in SEND_ORDER:
         gather(level)
+
     def place(products, targets, lives):
         def one(b, carry):
             total = acc[b]
@@ -257,15 +255,13 @@
     for wait in core_waits:
         wait.wait_recv()
     gsum[...] += gc[...]
-    for k in range(YS):
-        gbs[k] = gb[k] + gbc[k]
-        for i in range(XS):
-            first = k * 128 + i * 32
-            gs[k, i, 0:32, :] = gsum[first:first + 32, :].astype(BF16)
-            gs[k, i, 32:48, :] = jnp.concatenate([gbs[k], gbs[k]], axis=0).astype(BF16)
+    gbs[...] = gb[...] + gbc[...]
     grad_waits = []
     for n, (k, q) in enumerate(plane):
-        grad_waits.append(push(gs.at[y_to[q], x_to[k]], gr.at[n], gr.at[n], plane_dev[n]))
+        gs[n, 0:32, :] = gsum[rows(y_to[q] * 128 + x_to[k] * 32, 32), :].astype(BF16)
+        total = gbs[y_to[q]]
+        gs[n, 32:48, :] = jnp.concatenate([total, total], axis=0).astype(BF16)
+        grad_waits.append(push(gs.at[n], gr.at[n], gr.at[n], plane_dev[n]))
 
     for b in range(2):
         upr[2 * y + b] = du[b, rows(y * 128 + 64, 64), :]
@@ -353,6 +349,11 @@
 
     for level in (1, 2, 3):
         take_back(level)
+    take_back(4)
+    for b in range(NB):
+        lanes = slice(b * BLK, (b + 1) * BLK)
+        gfeat[:, lanes] = (gacc[:, lanes] + acc[b]).astype(BF16)
+    give(1, gfeat, gfeat_hbm)
 
     for wait in grad_waits:
         wait.wait_recv()
@@ -371,12 +372,6 @@
     assemble(fullc, 1 - core)
     give(2, gself, gself_hbm)
     give(3, gneigh, gneigh_hbm)
-
-    take_back(4)
-    for b in range(NB):
-        lanes = slice(b * BLK, (b + 1) * BLK)
-        gfeat[:, lanes] = (gacc[:, lanes] + acc[b]).astype(BF16)
-    give(1, gfeat, gfeat_hbm)
 
     for copy in sent:
         copy.wait_send()
@@ -457,7 +452,7 @@
             pltpu.VMEM((YS, 8, BLK), F32),
             pltpu.VMEM((YS, 8, BLK), F32),
             pltpu.VMEM((YS, 8, BLK), F32),
-            pltpu.VMEM((YS, XS, 48, BLK), BF16),
+            pltpu.VMEM((YS * XS - 1, 48, BLK), BF16),
             pltpu.VMEM((YS * XS - 1, 48, BLK), BF16),
             pltpu.VMEM((4, 16, BLK), F32),
             pltpu.VMEM((4, 16, BLK), BF16),

time: 67.7 us -> 66.8 us (0.987)
  Pallas kernels: 66.9 us -> 66 us
    pallas_call x1, Pallas kernels: 65.1 us -> 64.2 us  [on_device(): pl.pallas_call(functools.partial(kernel, 1.0 / math.sqrt(nodes)), out_sha...]
where the time goes in v4:
time: 66.8 us; the launch traced here: 66.6 us
  Pallas kernels  66 us (99%)
    pallas_call x1, Pallas kernels, on_device(): pl.pallas_call(functools.partial(kernel, 1.0 / math.sqrt(nodes)), out_sha...  64.2 us
    pallas_call x1, Pallas kernels, on_device(): pl.pallas_call(deliver, out_shape=shapes, in_specs=[anywhere] * 5, out_sp...  1.75 us

profile of v4, /device:TPU:1, one launch (start us, length us, event | category | flops | bytes accessed | tf_op | source)
XLA Modules:
  0.0 66.6 jit_solution(11745696300108397422)
XLA Ops:
  0.6 64.2 %shard_map.155 = (bf16[64,1024]{1,0:T(8,128)(2,1)}, bf16[64,1024]{1,0:T(8,128)(2,1)}, f32[64,256]{1,0:T(8,128)}, f32[64,256]{1,0:T(8,128)}, f32[1,64]{1,0:T(1,128)}) custom-call(s32[2,12]{1,0:T(2,128)} %bitcast.21, s32[4,7]{1,0:T(4,128)} %bitcast.19, s32[4,7]{1,0:T(4,128)} %bitcast.20, s32[1,7]{1,0:T(1,128)} %ccnt_in.1, bf16[64,1024]{1,0:T(8,128)(2,1)} %feat_in.1, ...), custom_call_target="tpu_custom_call" | custom-call | tf_op jit(solution)/shard_map/pallas_call | solution.py:409
  64.9 1.8 %shard_map.156 = (bf16[64,1024]{1,0:T(8,128)(2,1)}, bf16[64,1024]{1,0:T(8,128)(2,1)}, f32[64,256]{1,0:T(8,128)}, f32[64,256]{1,0:T(8,128)}, f32[1,64]{1,0:T(1,128)}) custom-call(bf16[64,1024]{1,0:T(8,128)(2,1)} %get-tuple-element.15.refs_0_, bf16[64,1024]{1,0:T(8,128)(2,1)} %get-tuple-element.16.refs_1_, f32[64,256]{1,0:T(8,128)} %get-tuple-element.17.refs_2_, ...), custom_call_target="tpu_custom_call" | custom-call | tf_op jit(solution)/shard_map/pallas_call | solution.py:483

commit v5 on v4

--- a/solution.py
+++ b/solution.py
@@ -173,6 +173,8 @@
     pl.semaphore_wait(barrier, len(greeted))
 
     forward = {SEND_ORDER[0]: send_level(SEND_ORDER[0], xs.at[SEND_ORDER[0]], xr[SEND_ORDER[0]])}
+    for level in SEND_ORDER[1:]:
+        forward[level] = send_level(level, xs.at[level], xr[level])
     early = []
     for k in range(1, YS):
         early.append(push(
@@ -181,8 +183,6 @@
         early.append(push(
             cb.at[pl.ds(2 * y_to[k], 2)], cot3.at[:, rows(y * 64, 64), :],
             cot3.at[:, rows(y_from[k] * 64, 64), :], y_dev[k]))
-    for level in SEND_ORDER[1:]:
-        forward[level] = send_level(level, xs.at[level], xr[level])
 
     for b in range(2):
         fa[b, rows(y * 128, 64), :] = fb[2 * y + b]
@@ -355,6 +355,14 @@
         gfeat[:, lanes] = (gacc[:, lanes] + acc[b]).astype(BF16)
     give(1, gfeat, gfeat_hbm)
 
+    def settle():
+        for copy in sent:
+            copy.wait_send()
+        sent.clear()
+
+    tile_sends = sent[-len(near):]
+    del sent[-len(near):]
+    settle()
     for wait in grad_waits:
         wait.wait_recv()
     half_wait = push(full, fullc, fullc, other_core)
@@ -368,13 +376,14 @@
                 dst[first:first + 8, lanes] = tiles[k, p]
 
     assemble(full, core)
+    for copy in tile_sends:
+        copy.wait_send()
     half_wait.wait_recv()
     assemble(fullc, 1 - core)
     give(2, gself, gself_hbm)
     give(3, gneigh, gneigh_hbm)
 
-    for copy in sent:
-        copy.wait_send()
+    settle()
     for copy in shipped:
         copy.wait()
 

time: 66.8 us -> 66.8 us (level)
  no operation moved by 1% of the time
where the time goes in v5:
time: 66.8 us; the launch traced here: 66.7 us
  Pallas kernels  66 us (99%)
    pallas_call x1, Pallas kernels, on_device(): pl.pallas_call(functools.partial(kernel, 1.0 / math.sqrt(nodes)), out_sha...  64.3 us
    pallas_call x1, Pallas kernels, on_device(): pl.pallas_call(deliver, out_shape=shapes, in_specs=[anywhere] * 5, out_sp...  1.75 us

profile of v5, /device:TPU:1, one launch (start us, length us, event | category | flops | bytes accessed | tf_op | source)
XLA Modules:
  0.0 66.7 jit_solution(10500945064062929354)
XLA Ops:
  0.6 64.3 %shard_map.155 = (bf16[64,1024]{1,0:T(8,128)(2,1)}, bf16[64,1024]{1,0:T(8,128)(2,1)}, f32[64,256]{1,0:T(8,128)}, f32[64,256]{1,0:T(8,128)}, f32[1,64]{1,0:T(1,128)}) custom-call(s32[2,12]{1,0:T(2,128)} %bitcast.21, s32[4,7]{1,0:T(4,128)} %bitcast.19, s32[4,7]{1,0:T(4,128)} %bitcast.20, s32[1,7]{1,0:T(1,128)} %ccnt_in.1, bf16[64,1024]{1,0:T(8,128)(2,1)} %feat_in.1, ...), custom_call_target="tpu_custom_call" | custom-call | tf_op jit(solution)/shard_map/pallas_call | solution.py:418
  64.9 1.8 %shard_map.156 = (bf16[64,1024]{1,0:T(8,128)(2,1)}, bf16[64,1024]{1,0:T(8,128)(2,1)}, f32[64,256]{1,0:T(8,128)}, f32[64,256]{1,0:T(8,128)}, f32[1,64]{1,0:T(1,128)}) custom-call(bf16[64,1024]{1,0:T(8,128)(2,1)} %get-tuple-element.15.refs_0_, bf16[64,1024]{1,0:T(8,128)(2,1)} %get-tuple-element.16.refs_1_, f32[64,256]{1,0:T(8,128)} %get-tuple-element.17.refs_2_, ...), custom_call_target="tpu_custom_call" | custom-call | tf_op jit(solution)/shard_map/pallas_call | solution.py:492
